TPU v7x, 32 devices: a whole 2x2x4 slice. The times are simulated.
32 devices in a mesh: depth: 8 (over z, x), rows: 4 (over y, core).
Axes of the slice: x: 2, y: 2, z: 4, core: 2. Of those that a mesh axis runs over, the one named last changes fastest.
Arguments:
- spectrum: bfloat16 [2, 4096, 4096], P(None, 'rows'), may hold values from -6 to 6
- plane_index: int32 [8], P('depth'), may hold values from 0 to 2047
- kernel_width: int32 [8], P('depth'), may hold values from 1 to 3
- focus_gain: float32 [8], P('depth'), may hold values from 0.5 to 30
Outputs:
- depth_map: float32 [256, 4096], P('rows', 'depth')
- focused: float32 [2, 256, 4096], P(None, 'rows', 'depth')
All inputs are finite; a program needn't handle non-finite values.
Results may differ from a plain program's by a relative error of at most 0.0003.
Values may be sent and summed in bfloat16 or wider, within the bound.
A program may use at most 192 MiB of HBM per device.

v0:
```python
from functools import partial
import math

import jax
import jax.numpy as jnp
from jax import lax
from jax.sharding import PartitionSpec as P

NX = 4096
RADIX = 64
Y_WIN = 256
DEPTHS = 2048
MAXWIDTH = 3


def with_halo(block, sides, width):
    for axis, dim in sides:
        count = lax.axis_size(axis)
        forward = [(i, i + 1) for i in range(count - 1)]
        backward = [(target, source) for source, target in forward]
        low = lax.ppermute(
            lax.slice_in_dim(block, block.shape[dim] - width, None, axis=dim), axis, forward
        )
        high = lax.ppermute(lax.slice_in_dim(block, 0, width, axis=dim), axis, backward)
        block = jnp.concatenate([low, block, high], axis=dim)
    return block


def line_phase(plane_index, freqs):
    signed = jnp.where(freqs < NX // 2, freqs, freqs - NX)
    square = signed * signed
    upper_part = (square // NX)[None, :]
    lower_part = (square % NX)[None, :]
    depth_col = plane_index[:, None]
    turns = (depth_col * lower_part + NX * (depth_col * upper_part % NX)) % (NX * NX)
    return turns.astype(jnp.float32) * (-2.0 * math.pi / (NX * NX))


def sobel_energy(padded):
    vertical = padded[..., :-2, :] + 2.0 * padded[..., 1:-1, :] + padded[..., 2:, :]
    across = vertical[..., :, 2:] - vertical[..., :, :-2]
    horizontal = padded[..., :, :-2] + 2.0 * padded[..., :, 1:-1] + padded[..., :, 2:]
    downward = horizontal[..., 2:, :] - horizontal[..., :-2, :]
    return across * across + downward * downward


def smooth_columns(energy, radius):
    extent = energy.shape[-1]
    padded = jnp.pad(energy, [(0, 0)] * (energy.ndim - 1) + [(MAXWIDTH, MAXWIDTH)])
    summed = jnp.zeros_like(energy)
    for offset in range(-MAXWIDTH, MAXWIDTH + 1):
        inside = (abs(offset) <= radius).astype(jnp.float32)
        summed = summed + inside * padded[..., MAXWIDTH + offset : MAXWIDTH + offset + extent]
    return summed / (2 * radius + 1).astype(jnp.float32)


def section_tables(out_blocks):
    counter = jnp.arange(RADIX, dtype=jnp.int32)
    first_turns = counter[:, None] * counter[None, :] % RADIX
    first_angle = first_turns.astype(jnp.float32) * (2.0 * math.pi / RADIX)
    twist_angle = (counter[:, None] * counter[None, :]).astype(jnp.float32) * (2.0 * math.pi / NX)
    kept_index = jnp.arange(out_blocks, dtype=jnp.int32)
    second_turns = counter[:, None] * kept_index[None, :] % RADIX
    second_angle = second_turns.astype(jnp.float32) * (2.0 * math.pi / RADIX)
    return (
        jnp.cos(first_angle),
        jnp.sin(first_angle),
        jnp.cos(twist_angle),
        jnp.sin(twist_angle),
        jnp.cos(second_angle),
        jnp.sin(second_angle),
    )


def complex_einsum(form, real_part, imag_part, table_real, table_imag):
    product = partial(jnp.einsum, form, precision=lax.Precision.HIGHEST)
    return (
        product(real_part, table_real) - product(imag_part, table_imag),
        product(real_part, table_imag) + product(imag_part, table_real),
    )


def transform_last(real_part, imag_part, out_blocks):
    leading = real_part.shape[:-1]
    tables = section_tables(out_blocks)
    shaped_real = real_part.reshape(leading + (RADIX, RADIX))
    shaped_imag = imag_part.reshape(leading + (RADIX, RADIX))
    section_real, section_imag = complex_einsum(
        "...dc,da->...ca", shaped_real, shaped_imag, tables[0], tables[1]
    )
    twisted_real = section_real * tables[2] - section_imag * tables[3]
    twisted_imag = section_real * tables[3] + section_imag * tables[2]
    final_real, final_imag = complex_einsum(
        "...ca,cb->...ba", twisted_real, twisted_imag, tables[4], tables[5]
    )
    new_shape = leading + (out_blocks * RADIX,)
    return (final_real.reshape(new_shape) / RADIX, final_imag.reshape(new_shape) / RADIX)


def transform_middle(real_part, imag_part, out_blocks):
    leading = real_part.shape[:-2]
    columns_n = real_part.shape[-1]
    tables = section_tables(out_blocks)
    shaped_real = real_part.reshape(leading + (RADIX, RADIX, columns_n))
    shaped_imag = imag_part.reshape(leading + (RADIX, RADIX, columns_n))
    section_real, section_imag = complex_einsum(
        "...dcw,da->...caw", shaped_real, shaped_imag, tables[0], tables[1]
    )
    twist_real = tables[2][:, :, None]
    twist_imag = tables[3][:, :, None]
    twisted_real = section_real * twist_real - section_imag * twist_imag
    twisted_imag = section_real * twist_imag + section_imag * twist_real
    final_real, final_imag = complex_einsum(
        "...caw,cb->...baw", twisted_real, twisted_imag, tables[4], tables[5]
    )
    new_shape = leading + (out_blocks * RADIX, columns_n)
    return (final_real.reshape(new_shape) / RADIX, final_imag.reshape(new_shape) / RADIX)


def rotate(spectra, plane_index, rows_freq, cols_freq):
    row_phase = line_phase(plane_index, rows_freq)
    col_phase = line_phase(plane_index, cols_freq)
    row_cos = jnp.cos(row_phase)[:, :, None]
    row_sin = jnp.sin(row_phase)[:, :, None]
    col_cos = jnp.cos(col_phase)[:, None, :]
    col_sin = jnp.sin(col_phase)[:, None, :]
    factor_real = row_cos * col_cos - row_sin * col_sin
    factor_imag = row_cos * col_sin + row_sin * col_cos
    real_in = spectra[0].astype(jnp.float32)
    imag_in = spectra[1].astype(jnp.float32)
    return (
        real_in * factor_real - imag_in * factor_imag,
        real_in * factor_imag + imag_in * factor_real,
    )


def shards(spectrum, plane_index, kernel_width, focus_gain):
    row_place = lax.axis_index("rows")
    swapped = lax.all_to_all(spectrum, "rows", split_axis=2, concat_axis=1, tiled=True)
    band_cols = swapped.shape[2]
    rows_freq = jnp.arange(NX, dtype=jnp.int32)
    cols_freq = row_place * band_cols + jnp.arange(band_cols, dtype=jnp.int32)
    real_rot, imag_rot = rotate(swapped, plane_index, rows_freq, cols_freq)
    real_mid, imag_mid = transform_middle(real_rot, imag_rot, Y_WIN // RADIX)
    real_part, imag_part = transform_last(
        lax.all_to_all(real_mid, "rows", split_axis=1, concat_axis=2, tiled=True),
        lax.all_to_all(imag_mid, "rows", split_axis=1, concat_axis=2, tiled=True),
        RADIX,
    )
    intensity = real_part * real_part + imag_part * imag_part
    rimmed = with_halo(intensity, (("rows", 1),), 1)
    padded = jnp.pad(rimmed, ((0, 0), (0, 0), (1, 1)))
    energy = sobel_energy(padded)
    smoothed = smooth_columns(energy, kernel_width[:, None, None])
    scores = focus_gain[:, None, None] * jnp.log(1.0 + smoothed)
    highest = jnp.max(scores, axis=0)
    weights = jnp.exp(scores - highest[None])
    depth_value = (plane_index.astype(jnp.float32) / DEPTHS)[:, None, None]
    summed = jnp.sum(weights, axis=0)
    depth_sum = jnp.sum(weights * depth_value, axis=0)
    real_sum = jnp.sum(weights * real_part, axis=0)
    imag_sum = jnp.sum(weights * imag_part, axis=0)
    gathered = (
        lax.all_to_all(highest[None], "depth", split_axis=2, concat_axis=0, tiled=True),
        lax.all_to_all(summed[None], "depth", split_axis=2, concat_axis=0, tiled=True),
        lax.all_to_all(depth_sum[None], "depth", split_axis=2, concat_axis=0, tiled=True),
        lax.all_to_all(real_sum[None], "depth", split_axis=2, concat_axis=0, tiled=True),
        lax.all_to_all(imag_sum[None], "depth", split_axis=2, concat_axis=0, tiled=True),
    )
    peak = jnp.max(gathered[0], axis=0)
    factors = jnp.exp(gathered[0] - peak[None])
    total_weight = jnp.sum(gathered[1] * factors, axis=0)
    total_depth = jnp.sum(gathered[2] * factors, axis=0)
    total_real = jnp.sum(gathered[3] * factors, axis=0)
    total_imag = jnp.sum(gathered[4] * factors, axis=0)
    depth_map = total_depth / total_weight
    focused = jnp.stack([total_real / total_weight, total_imag / total_weight])
    return (depth_map, focused)


def solution(mesh):
    return jax.shard_map(
        shards,
        mesh=mesh,
        in_specs=(P(None, "rows", None), P("depth"), P("depth"), P("depth")),
        out_specs=(P("rows", "depth"), P(None, "rows", "depth")),
        check_vma=False,
    )
```

profile of v0, /device:TPU:11, one launch (start us, length us, event | category | flops | bytes accessed | tf_op | source)
XLA Modules:
  0.0 823.1 jit_solution(6661758565761170029)
XLA Ops:
  0.6 41.7 %copy.112 = bf16[2,1024,4096]{1,0,2:T(2,128)(2,1)} copy(bf16[2,1024,4096]{2,1,0:T(8,128)(2,1)} %param.4) | data formatting | bytes 33554432 | tf_op args[0]
  42.3 7.6 all-to-all-start
  51.4 180.7 %all-to-all-done = bf16[2,1024,4096]{1,0,2:T(2,128)(2,1)} async-done(((bf16[2,1024,4096]{1,0,2:T(2,128)(2,1)}), bf16[2,1024,4096]{1,0,2:T(2,128)(2,1)}, u32[]{:S(2)}, u32[]{:S(2)}) %all-to-all-start) | async-done | bytes 16777248 | tf_op jit(solution)/shard_map/all_to_all | solution.py:139
  232.1 11.1 %copy.113 = bf16[2,1024,4096]{1,2,0:T(8,128)(2,1)S(1)} copy(bf16[2,1024,4096]{1,0,2:T(2,128)(2,1)} %all-to-all-done) | data formatting | bytes 33554432 | tf_op jit(solution)/shard_map/all_to_all | solution.py:139
  243.3 11.8 %slice_convert_fusion.1 = (f32[1,4,1024,1024]{2,3,1,0:T(8,128)}, f32[1,4,1024,1024]{2,3,1,0:T(8,128)}) fusion(bf16[2,4,1024,1024]{2,3,1,0:T(8,128)(2,1)S(1)} %bitcast.157), kind=kLoop, calls=%fused_computation.31 | loop fusion | flops 8388608 | bytes 50331648 | tf_op jit(solution)/shard_map/convert_element_type | solution.py:129
  255.1 16.4 %copy.114 = f32[1,4,1024,1024]{3,2,1,0:T(8,128)} copy(f32[1,4,1024,1024]{2,3,1,0:T(8,128)} %get-tuple-element.14) | data formatting | bytes 33554432 | tf_op jit(solution)/shard_map/convert_element_type | solution.py:129
  271.5 16.4 %copy.117 = f32[1,4,1024,1024]{3,2,1,0:T(8,128)} copy(f32[1,4,1024,1024]{2,3,1,0:T(8,128)} %get-tuple-element.15) | data formatting | bytes 33554432 | tf_op jit(solution)/shard_map/convert_element_type | solution.py:130
  287.9 22.1 %multiply_subtract_fusion = (f32[64,64,1024]{2,1,0:T(8,128)}, f32[64,64,1024]{2,1,0:T(8,128)}) fusion(f32[64,64,1024]{2,1,0:T(8,128)} %bitcast.156, f32[64,64,1024]{2,1,0:T(8,128)} %bitcast.155, f32[1024]{0:T(1024)S(1)} %get-tuple-element.24, f32[64,64]{1,0:T(8,128)S(1)} %copy.116, f32[1024]{0:T(1024)S(1)} %get-tuple-element.25, f32[64,64]{1,0:T(8,128)S(1)} %copy.115), kind=kLoop, calls=%fused_computation.9 | loop fusion | flops 50331648 | bytes 67149824 | tf_op jit(solution)/shard_map/sub | solution.py:132
  309.9 33.1 %fusion.14 = f32[64,64,1024]{2,0,1:T(8,128)} fusion(f32[64,64,1024]{2,1,0:T(8,128)} %get-tuple-element.11), kind=kOutput, calls=%fused_computation.22 | convolution fusion | flops 3221282816 | bytes 33554432 | tf_op jit(solution)/shard_map/...dcw,da->...caw/dot_general | solution.py:78
  343.0 33.6 %fusion.12 = f32[64,64,1024]{2,0,1:T(8,128)} fusion(f32[64,64,1024]{2,1,0:T(8,128)} %get-tuple-element.11), kind=kOutput, calls=%fused_computation.20 | convolution fusion | flops 3221282816 | bytes 33554432 | tf_op jit(solution)/shard_map/...dcw,da->...caw/dot_general | solution.py:79
  376.6 35.6 %fusion.20 = f32[64,64,1024]{2,0,1:T(8,128)} fusion(f32[64,64,1024]{2,0,1:T(8,128)} %fusion.14, f32[64,64,1024]{2,1,0:T(8,128)} %get-tuple-element.10), kind=kOutput, calls=%fused_computation.28 | convolution fusion | flops 3225477120 | bytes 50331648 | tf_op jit(solution)/shard_map/...dcw,da->...caw/dot_general | solution.py:78
  412.2 38.1 %fusion.1 = (f32[64,64,1024]{2,1,0:T(8,128)}, f32[64,64,1024]{2,1,0:T(8,128)}) fusion(f32[64,64,1024]{2,0,1:T(8,128)} %fusion.20, f32[64,64]{1,0:T(8,128)S(1)} %copy.123, f32[64,64]{1,0:T(8,128)S(1)} %copy.120, f32[64,64,1024]{2,0,1:T(8,128)} %fusion.12, f32[64,64,1024]{2,1,0:T(8,128)} %get-tuple-element.10), kind=kOutput, calls=%fused_computation.3 | convolution fusion | flops 3250642944 | bytes 83918848 | tf_op jit(solution)/shard_map/...dcw,da->...caw/dot_general | solution.py:79
  450.2 22.9 %fusion.4 = f32[4,64,1024]{2,0,1:T(4,128)S(1)} fusion(f32[64,64,1024]{2,1,0:T(8,128)} %get-tuple-element.13), kind=kOutput, calls=%fused_computation.12 | convolution fusion | flops 201330176 | bytes 17825792 | tf_op jit(solution)/shard_map/...caw,cb->...baw/dot_general | solution.py:79
  473.2 22.5 %fusion.6 = f32[4,64,1024]{2,0,1:T(4,128)S(1)} fusion(f32[64,64,1024]{2,1,0:T(8,128)} %get-tuple-element.13), kind=kOutput, calls=%fused_computation.14 | convolution fusion | flops 201330176 | bytes 17825792 | tf_op jit(solution)/shard_map/...caw,cb->...baw/dot_general | solution.py:78
  495.7 15.5 %fusion.35 = f32[4,64,1024]{2,0,1:T(4,128)S(1)} fusion(f32[4,64,1024]{2,0,1:T(4,128)S(1)} %fusion.6, f32[64,64,1024]{2,1,0:T(8,128)S(1)} %bitcast.154), kind=kOutput, calls=%fused_computation.51 | convolution fusion | flops 201854464 | bytes 18874368 | tf_op jit(solution)/shard_map/...caw,cb->...baw/dot_general | solution.py:78
  518.5 22.4 %fusion.32 = f32[4,64,1024]{2,0,1:T(4,128)S(1)} fusion(f32[4,64,1024]{2,0,1:T(4,128)S(1)} %fusion.4, f32[64,64,1024]{2,1,0:T(8,128)} %get-tuple-element.12), kind=kOutput, calls=%fused_computation.50 | convolution fusion | flops 201854464 | bytes 18874368 | tf_op jit(solution)/shard_map/...caw,cb->...baw/dot_general | solution.py:79
  565.6 6.0 convolution_subtract_fusion
  618.7 19.4 %reduce.5 = f32[4096,64]{1,0:T(8,128)} reduce(f32[4096,1,64]{2,1,0:T(1,128)S(1)} %bitcast.162, f32[]{:T(128)} %broadcast.1008), dimensions={1}, to_apply=%bitcast.136.reduce_sub_computation | reduce | bytes 2097156
  641.5 5.9 all-to-all-start.5
  652.3 19.4 %reduce.7 = f32[4096,64]{1,0:T(8,128)} reduce(f32[4096,1,64]{2,1,0:T(1,128)S(1)} %bitcast.163, f32[]{:T(128)} %broadcast.1008), dimensions={1}, to_apply=%bitcast.138.reduce_sub_computation | reduce | bytes 2097156
  685.3 19.4 %reduce.1 = f32[4096,64]{1,0:T(8,128)} reduce(f32[4096,1,64]{2,1,0:T(1,128)S(1)} %bitcast.164, f32[]{:T(128)} %broadcast.1008), dimensions={1}, to_apply=%bitcast.132.reduce_sub_computation | reduce | bytes 2097156
  716.3 19.4 %reduce.3 = f32[4096,64]{1,0:T(8,128)} reduce(f32[4096,1,64]{2,1,0:T(1,128)S(1)} %bitcast.165, f32[]{:T(128)} %broadcast.1008), dimensions={1}, to_apply=%bitcast.134.reduce_sub_computation | reduce | bytes 2097156
  747.1 19.4 %reduce.9 = f32[4096,64]{1,0:T(8,128)} reduce(f32[4096,1,64]{2,1,0:T(1,128)S(1)} %bitcast.166, f32[]{:T(128)} %broadcast.1008), dimensions={1}, to_apply=%bitcast.140.reduce_sub_computation | reduce | bytes 2097156
  769.8 5.8 all-to-all-start.3
  (105 shorter events, 173.8 us)
Async XLA Ops:
  42.3 189.8 %all-to-all-start = ((bf16[2,1024,4096]{1,0,2:T(2,128)(2,1)}), bf16[2,1024,4096]{1,0,2:T(2,128)(2,1)}, u32[]{:S(2)}, u32[]{:S(2)}) async-start(bf16[2,1024,4096]{1,0,2:T(2,128)(2,1)} %copy.112), calls=%async_computation | async-start | bytes 33554432 | tf_op jit(solution)/shard_map/all_to_all | solution.py:139
  450.2 45.5 %slice-start = ((s8[16777216]{0:T(1024)(128)(4,1)}), s8[4194304]{0:T(1024)(128)(4,1)S(1)}, s32[]{:S(2)}) async-start(s8[16777216]{0:T(1024)(128)(4,1)} %bitcast.153), calls=%async_computation.8 | async-start | bytes 8388608
  450.2 45.5 %slice-start.1 = ((s8[16777216]{0:T(1024)(128)(4,1)}), s8[4194304]{0:T(1024)(128)(4,1)S(1)}, s32[]{:S(2)}) async-start(s8[16777216]{0:T(1024)(128)(4,1)} %bitcast.153), calls=%async_computation.9 | async-start | bytes 8388608
  473.2 22.5 %slice-start.2 = ((s8[16777216]{0:T(1024)(128)(4,1)}), s8[4194304]{0:T(1024)(128)(4,1)S(1)}, s32[]{:S(2)}) async-start(s8[16777216]{0:T(1024)(128)(4,1)} %bitcast.153), calls=%async_computation.10 | async-start | bytes 8388608
  473.2 22.5 %slice-start.3 = ((s8[16777216]{0:T(1024)(128)(4,1)}), s8[4194304]{0:T(1024)(128)(4,1)S(1)}, s32[]{:S(2)}) async-start(s8[16777216]{0:T(1024)(128)(4,1)} %bitcast.153), calls=%async_computation.11 | async-start | bytes 8388608
  514.0 29.6 %all-to-all-start.1 = ((f32[1,256,1024]{2,0,1:T(1,128)}), f32[1,256,1024]{2,0,1:T(1,128)S(1)}, u32[]{:S(2)}, u32[]{:S(2)}) async-start(f32[1,256,1024]{2,0,1:T(1,128)} %copy.127), calls=%async_computation.1 | async-start | bytes 2097152 | tf_op jit(solution)/shard_map/all_to_all | solution.py:146
  543.6 18.0 %all-to-all-start.2 = ((f32[1,256,1024]{2,0,1:T(1,128)}), f32[1,256,1024]{2,0,1:T(1,128)}, u32[]{:S(2)}, u32[]{:S(2)}) async-start(f32[1,256,1024]{2,0,1:T(1,128)} %copy.134), calls=%async_computation.2 | async-start | bytes 2097152 | tf_op jit(solution)/shard_map/all_to_all | solution.py:147
  565.6 6.0 copy-start.1
  565.6 6.0 copy-start.5
  575.1 5.5 copy-start
  592.2 10.3 %copy-start.3 = (f32[64,64,64]{2,0,1:T(8,128)S(1)}, f32[64,64,64]{2,0,1:T(8,128)}, u32[]{:S(2)}) copy-start(f32[64,64,64]{2,0,1:T(8,128)} %add_multiply_fusion) | copy-start | bytes 3145732
  595.3 7.2 copy-start.2
  596.8 1.0 copy-start.6
  597.8 8.7 %collective-permute-start = (f32[1,1,4096]{2,1,0:T(1,128)S(1)}, f32[1,1,4096]{2,1,0:T(1,128)S(1)}, u32[]{:S(2)}, u32[]{:S(2)}) collective-permute-start(f32[1,1,4096]{2,1,0:T(1,128)S(1)} %get-tuple-element.19), channel_id=1, source_target_pairs={{0,1},{1,2},{2,3},{4,5},{5,6},{6,7},{8,9},{9,10},{10,11},{12,13},{... | collective-permute-start | bytes 49160 | tf_op jit(solution)/shard_map/ppermute | solution.py:21
  600.6 6.0 collective-permute-start.1
  604.3 2.2 copy-start.7
  608.6 2.7 copy-start.4
  641.5 33.5 %all-to-all-start.5 = ((f32[8,1,32768]{2,1,0:T(1,128)}), f32[8,1,32768]{2,1,0:T(1,128)}, u32[]{:S(2)}, u32[]{:S(2)}) async-start(f32[8,1,32768]{2,1,0:T(1,128)} %reshape.833), calls=%async_computation.5 | async-start | bytes 2097152 | tf_op jit(solution)/shard_map/all_to_all | solution.py:165
  675.0 33.0 %all-to-all-start.7 = ((f32[8,1,32768]{2,1,0:T(1,128)}), f32[8,1,32768]{2,1,0:T(1,128)}, u32[]{:S(2)}, u32[]{:S(2)}) async-start(f32[8,1,32768]{2,1,0:T(1,128)} %reshape.835), calls=%async_computation.7 | async-start | bytes 2097152 | tf_op jit(solution)/shard_map/all_to_all | solution.py:168
  708.0 31.1 %all-to-all-start.6 = ((f32[8,1,32768]{2,1,0:T(1,128)}), f32[8,1,32768]{2,1,0:T(1,128)}, u32[]{:S(2)}, u32[]{:S(2)}) async-start(f32[8,1,32768]{2,1,0:T(1,128)} %reshape.829), calls=%async_computation.6 | async-start | bytes 2097152 | tf_op jit(solution)/shard_map/all_to_all | solution.py:167
  735.6 8.9 %copy-start.8 = (f32[1,64,4096]{2,1,0:T(8,128)S(1)}, f32[1,64,4096]{2,1,0:T(8,128)}, u32[]{:S(2)}) copy-start(f32[1,64,4096]{2,1,0:T(8,128)} %get-tuple-element.8) | copy-start | bytes 3145732
  739.1 30.7 %all-to-all-start.4 = ((f32[8,1,32768]{2,1,0:T(1,128)}), f32[8,1,32768]{2,1,0:T(1,128)}, u32[]{:S(2)}, u32[]{:S(2)}) async-start(f32[8,1,32768]{2,1,0:T(1,128)} %reshape.831), calls=%async_computation.4 | async-start | bytes 2097152 | tf_op jit(solution)/shard_map/all_to_all | solution.py:164
  769.8 37.9 %all-to-all-start.3 = ((f32[8,1,32768]{2,1,0:T(1,128)}), f32[8,1,32768]{2,1,0:T(1,128)}, u32[]{:S(2)}, u32[]{:S(2)}) async-start(f32[8,1,32768]{2,1,0:T(1,128)} %reshape.837), calls=%async_computation.3 | async-start | bytes 2097152 | tf_op jit(solution)/shard_map/all_to_all | solution.py:166
where the time goes:
time: 834 us; the launch traced here: 823 us
  matrix products  257 us (31%)
  waiting for transfers between devices  182 us (22%)
  other arithmetic  168 us (20%)
  local copies, waits for them, and re-layouts  163 us (20%)
  starting transfers between devices  49.8 us (6%)
    all_to_all x1, waiting for transfers between devices, shards(): lax.all_to_all(spectrum, 'rows', split_axis=2, concat_axis=1, tiled=True)  181 us
    unnamed x6, other arithmetic  96.9 us
    unnamed x40, local copies, waits for them, and re-layouts  80.4 us
    dot_general x4, matrix products, complex_einsum(): product(real_part, table_imag) + product(imag_part, table_real)  68.6 us
    dot_general x4, matrix products, complex_einsum(): product(imag_part, table_real)  65.6 us
    dot_general x4, matrix products, complex_einsum(): product(imag_part, table_imag)  65.1 us
    dot_general x4, matrix products, complex_einsum(): product(real_part, table_real) - product(imag_part, table_imag)  57.9 us
    sub x1, other arithmetic, rotate(): real_in * factor_real - imag_in * factor_imag  22.1 us
  transfers between devices with their start and end apart: 10, of which 2 were waited for; matrix products, arithmetic and copies ran while one was open for 22% of the time, Pallas kernels for 0%

commit v1 on v0

v1 whole, which is shorter than its diff:
```python
from functools import partial
import math

import numpy as np
import jax
import jax.numpy as jnp
from jax import lax
from jax.experimental import pallas as pl
from jax.experimental.pallas import tpu as pltpu
from jax.sharding import PartitionSpec as P

NX = 4096
Y_WIN = 256
DEPTHS = 2048
MAXWIDTH = 3
LANES = 128
SLABS = NX // LANES
CORES = 2
LAG = 3
VMEM_BYTES = 56 * 1024 * 1024


def line_phase(plane, freqs):
    signed = jnp.where(freqs < NX // 2, freqs, freqs - NX)
    square = signed * signed
    turns = (plane * (square % NX) + NX * (plane * (square // NX) % NX)) % (NX * NX)
    return turns.astype(jnp.float32) * (-2.0 * math.pi / (NX * NX))


def row_table(plane, place, count):
    freqs_n = NX // count
    band = Y_WIN // count
    turns = np.arange(Y_WIN)[:, None] * np.arange(freqs_n)[None, :] % NX
    angle = turns * (2.0 * np.pi / NX)
    base_cos = jnp.asarray(np.cos(angle).astype(np.float32))
    base_sin = jnp.asarray(np.sin(angle).astype(np.float32))
    phase = line_phase(plane, place * freqs_n + jnp.arange(freqs_n, dtype=jnp.int32))
    start = place * freqs_n * jnp.arange(Y_WIN, dtype=jnp.int32) % NX
    start_angle = start.astype(jnp.float32) * (2.0 * math.pi / NX)
    col_cos, col_sin = jnp.cos(phase)[None, :], jnp.sin(phase)[None, :]
    row_cos, row_sin = jnp.cos(start_angle)[:, None], jnp.sin(start_angle)[:, None]
    turn_cos = row_cos * col_cos - row_sin * col_sin
    turn_sin = row_cos * col_sin + row_sin * col_cos
    real = base_cos * turn_cos - base_sin * turn_sin
    imag = base_cos * turn_sin + base_sin * turn_cos
    upper = jnp.concatenate([real, -imag], axis=1)
    lower = jnp.concatenate([imag, real], axis=1)
    table = jnp.stack([upper, lower]).reshape(2, count // CORES, CORES, band, 2 * freqs_n)
    table = table.transpose(2, 1, 0, 3, 4).reshape(2 * Y_WIN, 2 * freqs_n)
    first = lax.reduce_precision(table, 8, 7)
    return first.astype(jnp.bfloat16), (table - first).astype(jnp.bfloat16)


def row_kernel(count, chunks, first_ref, second_ref, spec_ref, out_ref,
               part, core_in, half, chip_in, a_send, a_recv, b_send, b_recv):
    chips = count // CORES
    step = pl.program_id(0)
    me = lax.axis_index("rows")
    core, chip = lax.rem(me, CORES), lax.div(me, CORES)
    half_rows = part.shape[1] // CORES
    block = half_rows // chips
    width = spec_ref.shape[1]
    partner = chip * CORES + 1 - core

    def other(hop):
        return lax.rem(chip + hop, chips)

    def core_copy(k):
        rows = pl.ds(pl.multiple_of((1 - core) * half_rows, half_rows), half_rows)
        return pltpu.make_async_remote_copy(
            src_ref=part.at[k, rows], dst_ref=core_in.at[k],
            send_sem=a_send.at[k], recv_sem=a_recv.at[k],
            device_id={"rows": partner}, device_id_type=pl.DeviceIdType.MESH)

    def chip_copy(k, hop):
        rows = pl.ds(pl.multiple_of(other(hop) * block, block), block)
        return pltpu.make_async_remote_copy(
            src_ref=half.at[k, rows], dst_ref=chip_in.at[k, hop - 1],
            send_sem=b_send.at[k, hop - 1], recv_sem=b_recv.at[k, hop - 1],
            device_id={"rows": other(hop) * CORES + core}, device_id_type=pl.DeviceIdType.MESH)

    @pl.when(step == 0)
    def _():
        barrier = pltpu.get_barrier_semaphore()
        pl.semaphore_signal(barrier, inc=1, device_id={"rows": partner},
                            device_id_type=pl.DeviceIdType.MESH)
        for hop in range(1, chips):
            pl.semaphore_signal(barrier, inc=1, device_id={"rows": other(hop) * CORES + core},
                                device_id_type=pl.DeviceIdType.MESH)
        pl.semaphore_wait(barrier, chips)

    @pl.when(step < chunks)
    def _():
        part[step] = (
            jnp.dot(first_ref[...], spec_ref[...], preferred_element_type=jnp.float32)
            + jnp.dot(second_ref[...], spec_ref[...], preferred_element_type=jnp.float32))
        core_copy(step).start()

    @pl.when(jnp.logical_and(step >= 1, step < chunks + 1))
    def _():
        k = step - 1
        core_copy(k).wait()
        rows = pl.ds(pl.multiple_of(core * half_rows, half_rows), half_rows)
        half[k] = part[k, rows] + core_in[k]
        for hop in range(1, chips):
            chip_copy(k, hop).start()

    @pl.when(step >= LAG)
    def _():
        k = step - LAG
        rows = pl.ds(pl.multiple_of(chip * block, block), block)
        for hop in range(1, chips):
            chip_copy(k, hop).wait()
        total = half[k, rows]
        for hop in range(1, chips):
            total = total + chip_in[k, hop - 1]
        out_ref[:, pl.ds(pl.multiple_of(k * width, width), width)] = total


def row_transform(spectra, first, second, count):
    depth = spectra.shape[0]
    width = 512
    chunks = NX // width
    chips = count // CORES
    half_rows = 2 * Y_WIN // CORES
    block = half_rows // chips
    whole = pl.BlockSpec((2 * Y_WIN, depth), lambda c: (0, 0))
    return pl.pallas_call(
        partial(row_kernel, count, chunks),
        out_shape=jax.ShapeDtypeStruct((block, NX), jnp.float32),
        grid=(chunks + LAG,),
        in_specs=[whole, whole,
                  pl.BlockSpec((depth, width), lambda c: (0, jnp.minimum(c, chunks - 1)))],
        out_specs=pl.BlockSpec((block, NX), lambda c: (0, 0)),
        scratch_shapes=[
            pltpu.VMEM((chunks, 2 * Y_WIN, width), jnp.float32),
            pltpu.VMEM((chunks, half_rows, width), jnp.float32),
            pltpu.VMEM((chunks, half_rows, width), jnp.float32),
            pltpu.VMEM((chunks, chips - 1, block, width), jnp.float32),
            pltpu.SemaphoreType.DMA((chunks,)),
            pltpu.SemaphoreType.DMA((chunks,)),
            pltpu.SemaphoreType.DMA((chunks, chips - 1)),
            pltpu.SemaphoreType.DMA((chunks, chips - 1)),
        ],
        compiler_params=pltpu.CompilerParams(
            collective_id=0, has_side_effects=True, vmem_limit_bytes=VMEM_BYTES),
    )(first, second, spectra)


def butterflies(real, imag):
    n = len(real)
    if n == 1:
        return real, imag
    even_r, even_i = butterflies(real[0::2], imag[0::2])
    odd_r, odd_i = butterflies(real[1::2], imag[1::2])
    out_r, out_i = [None] * n, [None] * n
    for k in range(n // 2):
        c, s = math.cos(2.0 * math.pi * k / n), math.sin(2.0 * math.pi * k / n)
        if k == 0:
            tr, ti = odd_r[k], odd_i[k]
        elif 4 * k == n:
            tr, ti = -odd_i[k], odd_r[k]
        else:
            tr, ti = odd_r[k] * c - odd_i[k] * s, odd_r[k] * s + odd_i[k] * c
        out_r[k], out_i[k] = even_r[k] + tr, even_i[k] + ti
        out_r[k + n // 2], out_i[k + n // 2] = even_r[k] - tr, even_i[k] - ti
    return out_r, out_i


def column_kernel(strip_ref, phase_ref, twist_ref, table_ref, pic_ref, power_ref, mid):
    band = strip_ref.shape[0] // 2

    @pl.loop(0, band // 8)
    def _(s):
        at = pl.multiple_of(s * 8, 8)
        real, imag = [], []
        for slab in range(SLABS):
            lanes = slice(slab * LANES, (slab + 1) * LANES)
            xr = strip_ref[pl.ds(at, 8), lanes]
            xi = strip_ref[pl.ds(band + at, 8), lanes]
            pc, ps = phase_ref[0:1, lanes], phase_ref[1:2, lanes]
            real.append(xr * pc - xi * ps)
            imag.append(xr * ps + xi * pc)
        real, imag = butterflies(real, imag)
        for slab in range(SLABS):
            tc, ts = twist_ref[0, slab:slab + 1, :], twist_ref[1, slab:slab + 1, :]
            mid[slab, pl.ds(at, 8), 0:LANES] = real[slab] * tc - imag[slab] * ts
            mid[slab, pl.ds(at, 8), LANES:2 * LANES] = real[slab] * ts + imag[slab] * tc

    per = 4

    @pl.loop(0, SLABS // per)
    def _(q):
        slabs = pl.ds(q * per, per)
        rows = mid[slabs].reshape(per * band, 2 * LANES)
        both = jnp.dot(rows, table_ref[...], precision=lax.Precision.HIGHEST,
                       preferred_element_type=jnp.float32)
        real, imag = both[:, :LANES], both[:, LANES:]
        pic_ref[0, slabs] = real.reshape(per, band, LANES)
        pic_ref[1, slabs] = imag.reshape(per, band, LANES)
        power_ref[slabs] = (real * real + imag * imag).reshape(per, band, LANES)


def column_transform(strip, phase):
    band = strip.shape[0] // 2
    lane = np.arange(LANES)
    twist = np.arange(SLABS)[:, None] * lane[None, :] * (2.0 * np.pi / NX)
    twist = np.stack([np.cos(twist), np.sin(twist)]).astype(np.float32)
    angle = lane[:, None] * lane[None, :] % LANES * (2.0 * np.pi / LANES)
    cosine, sine = np.cos(angle) / NX, np.sin(angle) / NX
    table = np.block([[cosine, sine], [-sine, cosine]]).astype(np.float32)
    return pl.pallas_call(
        column_kernel,
        out_shape=(jax.ShapeDtypeStruct((2, SLABS, band, LANES), jnp.float32),
                   jax.ShapeDtypeStruct((SLABS, band, LANES), jnp.float32)),
        scratch_shapes=[pltpu.VMEM((SLABS, band, 2 * LANES), jnp.float32)],
        compiler_params=pltpu.CompilerParams(vmem_limit_bytes=VMEM_BYTES),
    )(strip, phase, jnp.asarray(twist), jnp.asarray(table))


def wrapped(block, forward):
    lane = lax.broadcasted_iota(jnp.int32, block.shape, block.ndim - 1)
    shift = LANES - 1 if forward else 1
    edge = LANES - 1 if forward else 0
    return jnp.where(lane == edge, 0.0, pltpu.roll(block, shift, block.ndim - 1))


def score_kernel(groups, smooth_ref, power_ref, low_ref, high_ref, pic_ref, out_ref,
                 rim, energy, score):
    band = power_ref.shape[1]
    rim[1:SLABS + 1, 8:8 + band, :] = power_ref[...]
    rim[1:SLABS + 1, 7:8, :] = low_ref[...]
    rim[1:SLABS + 1, 8 + band:9 + band, :] = high_ref[...]
    rim[0, 7:9 + band, :] = wrapped(rim[SLABS, 7:9 + band, :], False)
    rim[SLABS + 1, 7:9 + band, :] = wrapped(rim[1, 7:9 + band, :], True)

    @pl.loop(0, SLABS)
    def _(slab):
        def vertical(j):
            return rim[j, 7:7 + band, :] + 2.0 * rim[j, 8:8 + band, :] + rim[j, 9:9 + band, :]

        def horizontal(top):
            rows = slice(top, top + band)
            return rim[slab, rows, :] + 2.0 * rim[slab + 1, rows, :] + rim[slab + 2, rows, :]

        across = vertical(slab + 2) - vertical(slab)
        downward = horizontal(9) - horizontal(7)
        energy[slab + MAXWIDTH] = across * across + downward * downward

    for k in range(MAXWIDTH):
        energy[k] = wrapped(energy[SLABS + k], False)
        energy[SLABS + MAXWIDTH + k] = wrapped(energy[MAXWIDTH + k], True)

    @pl.loop(0, SLABS)
    def _(slab):
        total = energy[slab + MAXWIDTH]
        for k in range(1, MAXWIDTH + 1):
            total = total + smooth_ref[0, k] * (
                energy[slab + MAXWIDTH - k] + energy[slab + MAXWIDTH + k])
        score[slab] = smooth_ref[0, 4] * jnp.log(1.0 + total / smooth_ref[0, 0])

    per = SLABS // groups
    piece = LANES // per

    @pl.loop(0, band // 8)
    def _(s):
        at = pl.multiple_of(s * 8, 8)
        block_of = lax.broadcasted_iota(jnp.int32, (8, LANES), 1) // piece
        for kind in range(3):
            for g in range(groups):
                held = []
                for i in range(per):
                    slab = g * per + i
                    if kind == 0:
                        held.append(score[slab, pl.ds(at, 8), :])
                    else:
                        held.append(pic_ref[kind - 1, slab, pl.ds(at, 8), :])
                gap = 1
                while gap < per:
                    low_lane = block_of // gap % 2 == 0
                    for i in range(per):
                        if i // gap % 2 == 0:
                            a, c = held[i], held[i + gap]
                            held[i] = jnp.where(low_lane, a, pltpu.roll(c, gap * piece, 1))
                            held[i + gap] = jnp.where(
                                low_lane, pltpu.roll(a, LANES - gap * piece, 1), c)
                    gap *= 2
                for d in range(per):
                    out_ref[d, pl.ds(kind * band + at, 8), g * LANES:(g + 1) * LANES] = held[d]

    for d in range(per):
        out_ref[d, 3 * band:3 * band + 8, :] = jnp.full((8, groups * LANES), smooth_ref[0, 5])


def score_records(smooth, power, low, high, pic, targets):
    band = power.shape[1]
    groups = SLABS // targets
    vmem = pl.BlockSpec(memory_space=pltpu.VMEM)
    return pl.pallas_call(
        partial(score_kernel, groups),
        out_shape=jax.ShapeDtypeStruct((targets, 3 * band + 8, groups * LANES), jnp.float32),
        in_specs=[pl.BlockSpec(memory_space=pltpu.SMEM), vmem, vmem, vmem, vmem],
        out_specs=vmem,
        scratch_shapes=[
            pltpu.VMEM((SLABS + 2, band + 16, LANES), jnp.float32),
            pltpu.VMEM((SLABS + 2 * MAXWIDTH, band, LANES), jnp.float32),
            pltpu.VMEM((SLABS, band, LANES), jnp.float32),
        ],
        compiler_params=pltpu.CompilerParams(vmem_limit_bytes=VMEM_BYTES),
    )(smooth, power, low, high, pic)


def merge_kernel(rec_ref, order_ref, map_ref, field_ref):
    planes, rows_all, _ = rec_ref.shape
    band = (rows_all - 8) // 3
    peak = rec_ref[0, 0:band, :]
    for p in range(1, planes):
        peak = jnp.maximum(peak, rec_ref[p, 0:band, :])
    summed = jnp.zeros_like(peak)
    totals = [jnp.zeros_like(peak) for _ in range(3)]
    for p in range(planes):
        weight = jnp.exp(rec_ref[p, 0:band, :] - peak)
        summed = summed + weight
        totals[0] = totals[0] + weight * rec_ref[p, 3 * band:3 * band + 1, :]
        totals[1] = totals[1] + weight * rec_ref[p, band:2 * band, :]
        totals[2] = totals[2] + weight * rec_ref[p, 2 * band:3 * band, :]
    merged = jnp.concatenate([total / summed for total in totals], axis=0)
    placed = jnp.zeros_like(merged)
    for _ in range(3):
        term = merged.astype(jnp.bfloat16)
        placed = placed + jnp.dot(term, order_ref[...], preferred_element_type=jnp.float32)
        merged = merged - term.astype(jnp.float32)
    map_ref[...] = placed[0:band]
    field_ref[0] = placed[band:2 * band]
    field_ref[1] = placed[2 * band:3 * band]


def merge(records):
    planes, rows_all, width = records.shape
    band = (rows_all - 8) // 3
    per = SLABS // (width // LANES)
    piece = LANES // per
    spot = np.arange(width)
    slab = spot // LANES * per + spot % LANES // piece
    order = np.zeros((width, width), np.float32)
    order[spot, spot % piece * SLABS + slab] = 1.0
    return pl.pallas_call(
        merge_kernel,
        out_shape=(jax.ShapeDtypeStruct((band, width), jnp.float32),
                   jax.ShapeDtypeStruct((2, band, width), jnp.float32)),
        compiler_params=pltpu.CompilerParams(vmem_limit_bytes=VMEM_BYTES),
    )(records, jnp.asarray(order, jnp.bfloat16))


def shards(spectrum, plane_index, kernel_width, focus_gain):
    count = lax.axis_size("rows")
    targets = lax.axis_size("depth")
    place = lax.axis_index("rows")
    plane, radius = plane_index[0], kernel_width[0]
    first, second = row_table(plane, place, count)
    spectra = spectrum.reshape(2 * spectrum.shape[1], NX)
    strip = row_transform(spectra, first, second, count)
    phase = line_phase(plane, jnp.arange(NX, dtype=jnp.int32))
    pic, power = column_transform(strip, jnp.stack([jnp.cos(phase), jnp.sin(phase)]))
    band = power.shape[1]
    forward = [(i, i + 1) for i in range(count - 1)]
    backward = [(i + 1, i) for i in range(count - 1)]
    low = lax.ppermute(power[:, band - 1:, :], "rows", forward)
    high = lax.ppermute(power[:, :1, :], "rows", backward)
    inside = (jnp.arange(1, MAXWIDTH + 1) <= radius).astype(jnp.float32)
    smooth = jnp.concatenate([
        (2 * radius + 1).astype(jnp.float32)[None], inside, focus_gain,
        plane_index.astype(jnp.float32) / DEPTHS])[None]
    records = score_records(smooth, power, low, high, pic, targets)
    records = lax.all_to_all(records, "depth", split_axis=0, concat_axis=0, tiled=True)
    return merge(records)


def solution(mesh):
    return jax.shard_map(
        shards,
        mesh=mesh,
        in_specs=(P(None, "rows", None), P("depth"), P("depth"), P("depth")),
        out_specs=(P("rows", "depth"), P(None, "rows", "depth")),
        check_vma=False,
    )
```

time: 834 us -> 179 us (0.21); the launches traced: 823 us -> 177 us
  matrix products: 257 us -> 0 us
  waiting for transfers between devices: 182 us -> 1.21 us
  local copies, waits for them, and re-layouts: 163 us -> 1.87 us
  other arithmetic: 168 us -> 7.8 us
  Pallas kernels: 0 us -> 80.7 us
  blocking collectives: 0 us -> 76.7 us
  starting transfers between devices: 49.8 us -> 5.55 us
    dot_general x16 -> x0, matrix products: 257 us -> none  [the longest x4 68.6 us: complex_einsum(): product(real_part, table_imag) + product(imag_part, table_real)]
    all_to_all x8 -> x0, waiting for transfers between devices: 182 us -> none  [the longest x1 181 us: shards(): lax.all_to_all(spectrum, 'rows', split_axis=2, concat_axis=1, tiled=True)]
    unnamed x6 -> x0, other arithmetic: 96.9 us -> none
    pallas_call x0 -> x4, Pallas kernels: none -> 80.7 us  [the longest x1 56.7 us: row_transform(): pl.pallas_call(partial(row_kernel, count, chunks), out_shape=jax.ShapeDty...]
    unnamed x40 -> x4, local copies, waits for them, and re-layouts: 80.4 us -> 0.61 us
    all_to_all x0 -> x1, blocking collectives: none -> 76.7 us  [shards(): lax.all_to_all(records, 'depth', split_axis=0, concat_axis=0, tiled=True)]
    all_to_all x8 -> x0, starting transfers between devices: 45.1 us -> none  [the longest x1 7.6 us: shards(): lax.all_to_all(spectrum, 'rows', split_axis=2, concat_axis=1, tiled=True)]
    convert_element_type x2 -> x0, local copies, waits for them, and re-layouts: 32.8 us -> none  [the longest x1 16.4 us: rotate(): real_in = spectra[0].astype(jnp.float32)]
  transfers between devices with their start and end apart: 10 -> 2, of which waited for: 2 -> 1; matrix products, arithmetic and copies ran while one was open for 22% -> 0% of each run, Pallas kernels for 0% -> 0%
where the time goes in v1:
time: 179 us; the launch traced here: 177 us
  Pallas kernels  80.7 us (45%)
  blocking collectives  76.7 us (43%)
  other arithmetic  7.8 us (4%)
  starting transfers between devices  5.55 us (3%)
  between operations  2.65 us (1%)
  local copies, waits for them, and re-layouts  1.87 us (1%)
    all_to_all x1, blocking collectives, shards(): lax.all_to_all(records, 'depth', split_axis=0, concat_axis=0, tiled=True)  76.7 us
    pallas_call x1, Pallas kernels, row_transform(): pl.pallas_call(partial(row_kernel, count, chunks), out_shape=jax.ShapeDty...  56.7 us
    pallas_call x1, Pallas kernels, score_records(): pl.pallas_call(partial(score_kernel, groups), out_shape=jax.ShapeDtypeStr...  13 us
    pallas_call x1, Pallas kernels, column_transform(): pl.pallas_call(column_kernel, out_shape=(jax.ShapeDtypeStruct((2, SLABS,...  7.44 us
    ppermute x1, starting transfers between devices, shards(): low = lax.ppermute(power[:, band - 1:, :], 'rows', forward)  3.63 us
    pallas_call x1, Pallas kernels, merge(): pl.pallas_call(merge_kernel, out_shape=(jax.ShapeDtypeStruct((band, width...  3.59 us
  transfers between devices with their start and end apart: 2, of which 1 were waited for; matrix products, arithmetic and copies ran while one was open for 0% of the time, Pallas kernels for 0%

profile of v1, /device:TPU:11, one launch (start us, length us, event | category | flops | bytes accessed | tf_op | source)
XLA Modules:
  0.0 176.6 jit_solution(5232396177153092253)
XLA Ops:
  1.3 0.1 fusion.27
  1.3 0.1 fusion.22
  1.4 2.1 %fusion.29 = (f32[256,1024]{1,0:T(8,128)S(1)}, f32[256,1024]{1,0:T(8,128)S(1)}, f32[256,1024]{1,0:T(8,128)S(1)}) fusion(f32[256,1024]{1,0:T(8,128)} %constant.116.clone, f32[256,1024]{1,0:T(8,128)} %constant.115.clone, f32[1024]{0:T(1024)S(1)} %get-tuple-element.16, f32[256]{0:T(256)S(1)} %get-tuple-element.17, f32[1024]{0:T(1024)S(1)} %get-tuple-element.15, ...), kind=kLoop, calls=%fused_computation.69 | loop fusion | flops 3407872 | bytes 5253120 | tf_op jit(solution)/shard_map/neg | solution.py:46
  3.5 0.5 pad_maximum_fusion
  4.0 0.3 maximum_bitcast_fusion
  4.3 0.3 copy.11
  4.5 2.9 %fusion = (bf16[512,2048]{1,0:T(8,128)(2,1)}, bf16[512,2048]{1,0:T(8,128)(2,1)}) fusion(f32[2,2,2,64,2048]{4,3,2,1,0:T(8,128)S(1)} %copy.11), kind=kLoop, calls=%fused_computation.2 | loop fusion | flops 4194304 | bytes 8388608 | tf_op jit(solution)/shard_map/convert_element_type | solution.py:51
  7.4 0.7 fusion.9
  8.1 0.7 pad_maximum_fusion.2.phase_ref
  8.8 56.7 %shard_map.104.strip_ref = f32[128,4096]{1,0:T(8,128)} custom-call(bf16[512,2048]{1,0:T(8,128)(2,1)} %get-tuple-element.7.first_ref, bf16[512,2048]{1,0:T(8,128)(2,1)} %get-tuple-element.6.second_ref, bf16[2048,4096]{1,0:T(8,128)(2,1)} %bitcast.17), custom_call_target="tpu_custom_call" | custom-call | tf_op jit(solution)/shard_map/pallas_call | solution.py:128
  65.5 7.4 %shard_map.105 = (f32[2,32,64,128]{3,2,1,0:T(8,128)}, f32[32,64,128]{2,1,0:T(8,128)}) custom-call(f32[128,4096]{1,0:T(8,128)} %shard_map.104.strip_ref, f32[2,4096]{1,0:T(2,128)} %pad_maximum_fusion.2.phase_ref, f32[2,32,128]{2,1,0:T(8,128)} %constant.117.clone.twist_ref, f32[256,256]{1,0:T(8,128)} %constant.118.clone.table_ref), custom_call_target="tpu_custom_call" | custom-call | tf_op jit(solution)/shard_map/pallas_call | solution.py:212
  72.9 1.0 fusion.30
  73.9 3.6 %collective-permute-start = (f32[32,1,128]{2,1,0:T(1,128)S(1)}, f32[32,1,128]{2,1,0:T(1,128)S(1)}, u32[]{:S(2)}, u32[]{:S(2)}) collective-permute-start(f32[32,1,128]{2,1,0:T(1,128)S(1)} %get-tuple-element.12), channel_id=1, source_target_pairs={{0,1},{1,2},{2,3},{4,5},{5,6},{6,7},{8,9},{9,10},{10,11},{12,13},{... | collective-permute-start | bytes 49160 | tf_op jit(solution)/shard_map/ppermute | solution.py:368
  77.6 1.9 %collective-permute-start.1 = (f32[32,1,128]{2,1,0:T(1,128)S(1)}, f32[32,1,128]{2,1,0:T(1,128)S(1)}, u32[]{:S(2)}, u32[]{:S(2)}) collective-permute-start(f32[32,1,128]{2,1,0:T(1,128)S(1)} %get-tuple-element.11), channel_id=1, source_target_pairs={{1,0},{2,1},{3,2},{5,4},{6,5},{7,6},{9,8},{10,9},{11,10},{13,12},{... | collective-permute-start | bytes 49160 | tf_op jit(solution)/shard_map/ppermute | solution.py:369
  80.8 0.6 maximum_bitcast_fusion.1.smooth_ref
  81.4 0.0 collective-permute-done.low_ref
  81.4 0.0 copy-start
  81.4 1.2 collective-permute-done.1.high_ref
  82.6 0.0 copy-start.1
  82.6 0.0 copy-done
  82.6 0.6 copy-done.1
  83.2 13.0 %shard_map.106 = f32[8,200,512]{2,1,0:T(8,128)} custom-call(f32[1,6]{1,0:T(1,128)} %maximum_bitcast_fusion.1.smooth_ref, f32[32,64,128]{2,1,0:T(8,128)} %get-tuple-element.4.power_ref, f32[32,1,128]{2,1,0:T(1,128)} %copy-done, f32[32,1,128]{2,1,0:T(1,128)} %copy-done.1, f32[2,32,64,128]{3,2,1,0:T(8,128)} %get-tuple-element.5.pic_ref), custom_call_target="tpu_custom_call" | custom-call | tf_op jit(solution)/shard_map/pallas_call | solution.py:299
  96.2 76.7 %all_to_all.5.rec_ref = f32[8,200,512]{2,1,0:T(8,128)} all-to-all(f32[8,200,512]{2,1,0:T(8,128)} %shard_map.106), channel_id=1, replica_groups=mesh['depth'=8,'rows'=4] {'depth'}, dimensions={0} | all-to-all | bytes 6553600 | tf_op jit(solution)/shard_map/all_to_all | solution.py:375
  173.0 3.6 %shard_map.107 = (f32[64,512]{1,0:T(8,128)}, f32[2,64,512]{2,1,0:T(8,128)}) custom-call(f32[8,200,512]{2,1,0:T(8,128)} %all_to_all.5.rec_ref, bf16[512,512]{1,0:T(8,128)(2,1)} %constant.119.clone.order_ref), custom_call_target="tpu_custom_call" | custom-call | tf_op jit(solution)/shard_map/pallas_call | solution.py:347
  (1 shorter events, 0.0 us)
Async XLA Ops:
  73.9 7.5 %collective-permute-start = (f32[32,1,128]{2,1,0:T(1,128)S(1)}, f32[32,1,128]{2,1,0:T(1,128)S(1)}, u32[]{:S(2)}, u32[]{:S(2)}) collective-permute-start(f32[32,1,128]{2,1,0:T(1,128)S(1)} %get-tuple-element.12), channel_id=1, source_target_pairs={{0,1},{1,2},{2,3},{4,5},{5,6},{6,7},{8,9},{9,10},{10,11},{12,13},{... | collective-permute-start | bytes 49160 | tf_op jit(solution)/shard_map/ppermute | solution.py:368
  77.6 5.1 %collective-permute-start.1 = (f32[32,1,128]{2,1,0:T(1,128)S(1)}, f32[32,1,128]{2,1,0:T(1,128)S(1)}, u32[]{:S(2)}, u32[]{:S(2)}) collective-permute-start(f32[32,1,128]{2,1,0:T(1,128)S(1)} %get-tuple-element.11), channel_id=1, source_target_pairs={{1,0},{2,1},{3,2},{5,4},{6,5},{7,6},{9,8},{10,9},{11,10},{13,12},{... | collective-permute-start | bytes 49160 | tf_op jit(solution)/shard_map/ppermute | solution.py:369
  81.4 1.2 copy-start
  82.6 0.6 copy-start.1

commit v2 on v1

--- a/solution.py
+++ b/solution.py
@@ -17,6 +17,9 @@
 SLABS = NX // LANES
 CORES = 2
 LAG = 3
+STRIP = 16
+STEPS = 32767.0
+TINY = 1e-33
 VMEM_BYTES = 56 * 1024 * 1024
 
 
@@ -225,131 +228,234 @@
     return jnp.where(lane == edge, 0.0, pltpu.roll(block, shift, block.ndim - 1))
 
 
-def score_kernel(groups, smooth_ref, power_ref, low_ref, high_ref, pic_ref, out_ref,
-                 rim, energy, score):
+def focus_kernel(groups, count, smooth_ref, power_ref, pic_ref, order_ref, map_ref, field_ref,
+                 rim, energy, score, send_s, send_q, send_r, recv_s, recv_q, recv_r,
+                 halo_send, halo_recv, sends, recvs):
     band = power_ref.shape[1]
-    rim[1:SLABS + 1, 8:8 + band, :] = power_ref[...]
-    rim[1:SLABS + 1, 7:8, :] = low_ref[...]
-    rim[1:SLABS + 1, 8 + band:9 + band, :] = high_ref[...]
-    rim[0, 7:9 + band, :] = wrapped(rim[SLABS, 7:9 + band, :], False)
-    rim[SLABS + 1, 7:9 + band, :] = wrapped(rim[1, 7:9 + band, :], True)
-
-    @pl.loop(0, SLABS)
-    def _(slab):
-        def vertical(j):
-            return rim[j, 7:7 + band, :] + 2.0 * rim[j, 8:8 + band, :] + rim[j, 9:9 + band, :]
-
-        def horizontal(top):
-            rows = slice(top, top + band)
-            return rim[slab, rows, :] + 2.0 * rim[slab + 1, rows, :] + rim[slab + 2, rows, :]
-
-        across = vertical(slab + 2) - vertical(slab)
-        downward = horizontal(9) - horizontal(7)
-        energy[slab + MAXWIDTH] = across * across + downward * downward
-
-    for k in range(MAXWIDTH):
-        energy[k] = wrapped(energy[SLABS + k], False)
-        energy[SLABS + MAXWIDTH + k] = wrapped(energy[MAXWIDTH + k], True)
-
-    @pl.loop(0, SLABS)
-    def _(slab):
-        total = energy[slab + MAXWIDTH]
-        for k in range(1, MAXWIDTH + 1):
-            total = total + smooth_ref[0, k] * (
-                energy[slab + MAXWIDTH - k] + energy[slab + MAXWIDTH + k])
-        score[slab] = smooth_ref[0, 4] * jnp.log(1.0 + total / smooth_ref[0, 0])
-
+    strips = band // STRIP
     per = SLABS // groups
     piece = LANES // per
-
-    @pl.loop(0, band // 8)
-    def _(s):
-        at = pl.multiple_of(s * 8, 8)
-        block_of = lax.broadcasted_iota(jnp.int32, (8, LANES), 1) // piece
-        for kind in range(3):
-            for g in range(groups):
-                held = []
+    width = groups * LANES
+    place, me = lax.axis_index("rows"), lax.axis_index("depth")
+    has_low, has_high = place > 0, place < count - 1
+
+    def halo(kind):
+        low = kind == 0
+        return pltpu.make_async_remote_copy(
+            src_ref=power_ref.at[:, pl.ds(0 if low else band - 8, 8)],
+            dst_ref=rim.at[pl.ds(1, SLABS), pl.ds(8 + band if low else 0, 8)],
+            send_sem=halo_send.at[kind], recv_sem=halo_recv.at[kind],
+            device_id={"rows": lax.rem(place + (count - 1 if low else 1), count)},
+            device_id_type=pl.DeviceIdType.MESH)
+
+    def copies(s, hop):
+        target = lax.rem(me + hop, per)
+        return [pltpu.make_async_remote_copy(
+            src_ref=src.at[s, target], dst_ref=dst.at[s, hop - 1],
+            send_sem=sends.at[s, hop - 1, i], recv_sem=recvs.at[s, hop - 1, i],
+            device_id={"depth": target}, device_id_type=pl.DeviceIdType.MESH)
+            for i, (src, dst) in enumerate(
+                ((send_s, recv_s), (send_q, recv_q), (send_r, recv_r)))]
+
+    barrier = pltpu.get_barrier_semaphore()
+
+    @pl.when(has_low)
+    def _():
+        pl.semaphore_signal(barrier, inc=1, device_id={"rows": place - 1},
+                            device_id_type=pl.DeviceIdType.MESH)
+
+    @pl.when(has_high)
+    def _():
+        pl.semaphore_signal(barrier, inc=1, device_id={"rows": place + 1},
+                            device_id_type=pl.DeviceIdType.MESH)
+
+    @pl.loop(1, per)
+    def _(hop):
+        pl.semaphore_signal(barrier, inc=1, device_id={"depth": lax.rem(me + hop, per)},
+                            device_id_type=pl.DeviceIdType.MESH)
+
+    pl.semaphore_wait(barrier, per - 1 + has_low.astype(jnp.int32) + has_high.astype(jnp.int32))
+
+    @pl.when(has_low)
+    def _():
+        halo(0).start()
+
+    @pl.when(has_high)
+    def _():
+        halo(1).start()
+
+    rim[1:SLABS + 1, 8:8 + band, :] = power_ref[...]
+
+    @pl.when(place == 0)
+    def _():
+        rim[1:SLABS + 1, 0:8, :] = jnp.zeros((SLABS, 8, LANES), jnp.float32)
+
+    @pl.when(place == count - 1)
+    def _():
+        rim[1:SLABS + 1, 8 + band:16 + band, :] = jnp.zeros((SLABS, 8, LANES), jnp.float32)
+
+    @pl.loop(0, strips)
+    def _(turn):
+        s = lax.rem(turn + 1, strips)
+        at = pl.multiple_of(s * STRIP, STRIP)
+
+        @pl.when(turn == max(strips - 2, 0))
+        def _():
+            @pl.when(has_low)
+            def _():
+                halo(0).wait_send()
+                halo(1).wait_recv()
+
+            @pl.when(has_high)
+            def _():
+                halo(1).wait_send()
+                halo(0).wait_recv()
+
+        window = pl.ds(at, STRIP + 16)
+        rim[0, window, :] = wrapped(rim[SLABS, window, :], False)
+        rim[SLABS + 1, window, :] = wrapped(rim[1, window, :], True)
+
+        @pl.loop(0, SLABS)
+        def _(slab):
+            before, here, after = (rim[slab + j, window, :] for j in range(3))
+
+            def vertical(x):
+                return x[7:7 + STRIP] + 2.0 * x[8:8 + STRIP] + x[9:9 + STRIP]
+
+            across = vertical(after) - vertical(before)
+            horizontal = before + 2.0 * here + after
+            downward = horizontal[9:9 + STRIP] - horizontal[7:7 + STRIP]
+            energy[slab + MAXWIDTH] = across * across + downward * downward
+
+        for k in range(MAXWIDTH):
+            energy[k] = wrapped(energy[SLABS + k], False)
+            energy[SLABS + MAXWIDTH + k] = wrapped(energy[MAXWIDTH + k], True)
+
+        @pl.loop(0, SLABS)
+        def _(slab):
+            total = energy[slab + MAXWIDTH]
+            for k in range(1, MAXWIDTH + 1):
+                total = total + smooth_ref[0, k] * (
+                    energy[slab + MAXWIDTH - k] + energy[slab + MAXWIDTH + k])
+            score[slab] = smooth_ref[0, 4] * jnp.log(1.0 + total / smooth_ref[0, 0])
+
+        block_of = lax.broadcasted_iota(jnp.int32, (STRIP, LANES), 1) // piece
+
+        def exchanged(held):
+            gap = 1
+            while gap < per:
+                low_lane = block_of // gap % 2 == 0
                 for i in range(per):
-                    slab = g * per + i
-                    if kind == 0:
-                        held.append(score[slab, pl.ds(at, 8), :])
-                    else:
-                        held.append(pic_ref[kind - 1, slab, pl.ds(at, 8), :])
-                gap = 1
-                while gap < per:
-                    low_lane = block_of // gap % 2 == 0
-                    for i in range(per):
-                        if i // gap % 2 == 0:
-                            a, c = held[i], held[i + gap]
-                            held[i] = jnp.where(low_lane, a, pltpu.roll(c, gap * piece, 1))
-                            held[i + gap] = jnp.where(
-                                low_lane, pltpu.roll(a, LANES - gap * piece, 1), c)
-                    gap *= 2
-                for d in range(per):
-                    out_ref[d, pl.ds(kind * band + at, 8), g * LANES:(g + 1) * LANES] = held[d]
-
-    for d in range(per):
-        out_ref[d, 3 * band:3 * band + 8, :] = jnp.full((8, groups * LANES), smooth_ref[0, 5])
-
-
-def score_records(smooth, power, low, high, pic, targets):
+                    if i // gap % 2 == 0:
+                        a, c = held[i], held[i + gap]
+                        held[i] = jnp.where(low_lane, a, pltpu.roll(c, gap * piece, 1))
+                        held[i + gap] = jnp.where(
+                            low_lane, pltpu.roll(a, LANES - gap * piece, 1), c)
+                gap *= 2
+            return held
+
+        @pl.loop(0, groups)
+        def _(g):
+            lanes = pl.ds(pl.multiple_of(g * LANES, LANES), LANES)
+            held = exchanged([score[g * per + i] for i in range(per)])
+            for d in range(per):
+                send_s[s, d, :, lanes] = held[d]
+            real, imag = (
+                exchanged([pic_ref[part, g * per + i, pl.ds(at, STRIP), :] for i in range(per)])
+                for part in range(2))
+            for d in range(per):
+                largest = jnp.max(jnp.maximum(jnp.abs(real[d]), jnp.abs(imag[d])),
+                                  axis=0, keepdims=True)
+                largest = jnp.maximum(largest, TINY)
+                send_r[s, d, :, lanes] = largest * (1.0 / STEPS)
+                scale = STEPS / largest
+                for part, value in ((0, real[d]), (1, imag[d])):
+                    level = jnp.floor(value * scale + 0.5).astype(jnp.int32)
+                    send_q[s, d, part * STRIP:(part + 1) * STRIP, lanes] = level.astype(jnp.int16)
+
+        for d in range(per):
+            send_r[s, d, :, width:width + LANES] = jnp.full((1, LANES), smooth_ref[0, 5])
+
+        @pl.loop(1, per)
+        def _(hop):
+            for copy in copies(s, hop):
+                copy.start()
+
+        recv_s[s, per - 1] = send_s[s, me]
+        recv_q[s, per - 1] = send_q[s, me]
+        recv_r[s, per - 1] = send_r[s, me]
+
+    @pl.loop(0, strips)
+    def _(turn):
+        s = lax.rem(turn + 1, strips)
+        at = pl.multiple_of(s * STRIP, STRIP)
+
+        @pl.loop(1, per)
+        def _(hop):
+            for copy in copies(s, hop):
+                copy.wait()
+
+        peak = recv_s[s, 0]
+        for p in range(1, per):
+            peak = jnp.maximum(peak, recv_s[s, p])
+        summed = jnp.zeros_like(peak)
+        totals = [jnp.zeros_like(peak) for _ in range(3)]
+        for p in range(per):
+            weight = jnp.exp(recv_s[s, p] - peak)
+            summed = summed + weight
+            totals[0] = totals[0] + weight * recv_r[s, p, :, width:width + 1]
+            scaled = weight * recv_r[s, p, :, 0:width]
+            for part in range(2):
+                level = recv_q[s, p, part * STRIP:(part + 1) * STRIP, :]
+                totals[1 + part] = totals[1 + part] + scaled * level.astype(jnp.int32).astype(
+                    jnp.float32)
+        merged = jnp.concatenate([total / summed for total in totals], axis=0)
+        placed = jnp.zeros_like(merged)
+        for _ in range(3):
+            term = merged.astype(jnp.bfloat16)
+            placed = placed + jnp.dot(term, order_ref[...], preferred_element_type=jnp.float32)
+            merged = merged - term.astype(jnp.float32)
+        rows = pl.ds(at, STRIP)
+        map_ref[rows, :] = placed[0:STRIP]
+        field_ref[0, rows, :] = placed[STRIP:2 * STRIP]
+        field_ref[1, rows, :] = placed[2 * STRIP:3 * STRIP]
+
+
+def focus(smooth, power, pic, targets, count):
     band = power.shape[1]
+    strips = band // STRIP
     groups = SLABS // targets
+    width = groups * LANES
+    piece = LANES // targets
+    spot = np.arange(width)
+    slab = spot // LANES * targets + spot % LANES // piece
+    order = np.zeros((width, width), np.float32)
+    order[spot, spot % piece * SLABS + slab] = 1.0
     vmem = pl.BlockSpec(memory_space=pltpu.VMEM)
+    records = [
+        pltpu.VMEM((strips, targets, STRIP, width), jnp.float32),
+        pltpu.VMEM((strips, targets, 2 * STRIP, width), jnp.int16),
+        pltpu.VMEM((strips, targets, 1, width + LANES), jnp.float32),
+    ]
     return pl.pallas_call(
-        partial(score_kernel, groups),
-        out_shape=jax.ShapeDtypeStruct((targets, 3 * band + 8, groups * LANES), jnp.float32),
-        in_specs=[pl.BlockSpec(memory_space=pltpu.SMEM), vmem, vmem, vmem, vmem],
-        out_specs=vmem,
+        partial(focus_kernel, groups, count),
+        out_shape=(jax.ShapeDtypeStruct((band, width), jnp.float32),
+                   jax.ShapeDtypeStruct((2, band, width), jnp.float32)),
+        in_specs=[pl.BlockSpec(memory_space=pltpu.SMEM), vmem, vmem, vmem],
+        out_specs=(vmem, vmem),
         scratch_shapes=[
             pltpu.VMEM((SLABS + 2, band + 16, LANES), jnp.float32),
-            pltpu.VMEM((SLABS + 2 * MAXWIDTH, band, LANES), jnp.float32),
-            pltpu.VMEM((SLABS, band, LANES), jnp.float32),
+            pltpu.VMEM((SLABS + 2 * MAXWIDTH, STRIP, LANES), jnp.float32),
+            pltpu.VMEM((SLABS, STRIP, LANES), jnp.float32),
+            *records, *records,
+            pltpu.SemaphoreType.DMA((2,)),
+            pltpu.SemaphoreType.DMA((2,)),
+            pltpu.SemaphoreType.DMA((strips, targets - 1, 3)),
+            pltpu.SemaphoreType.DMA((strips, targets - 1, 3)),
         ],
-        compiler_params=pltpu.CompilerParams(vmem_limit_bytes=VMEM_BYTES),
-    )(smooth, power, low, high, pic)
-
-
-def merge_kernel(rec_ref, order_ref, map_ref, field_ref):
-    planes, rows_all, _ = rec_ref.shape
-    band = (rows_all - 8) // 3
-    peak = rec_ref[0, 0:band, :]
-    for p in range(1, planes):
-        peak = jnp.maximum(peak, rec_ref[p, 0:band, :])
-    summed = jnp.zeros_like(peak)
-    totals = [jnp.zeros_like(peak) for _ in range(3)]
-    for p in range(planes):
-        weight = jnp.exp(rec_ref[p, 0:band, :] - peak)
-        summed = summed + weight
-        totals[0] = totals[0] + weight * rec_ref[p, 3 * band:3 * band + 1, :]
-        totals[1] = totals[1] + weight * rec_ref[p, band:2 * band, :]
-        totals[2] = totals[2] + weight * rec_ref[p, 2 * band:3 * band, :]
-    merged = jnp.concatenate([total / summed for total in totals], axis=0)
-    placed = jnp.zeros_like(merged)
-    for _ in range(3):
-        term = merged.astype(jnp.bfloat16)
-        placed = placed + jnp.dot(term, order_ref[...], preferred_element_type=jnp.float32)
-        merged = merged - term.astype(jnp.float32)
-    map_ref[...] = placed[0:band]
-    field_ref[0] = placed[band:2 * band]
-    field_ref[1] = placed[2 * band:3 * band]
-
-
-def merge(records):
-    planes, rows_all, width = records.shape
-    band = (rows_all - 8) // 3
-    per = SLABS // (width // LANES)
-    piece = LANES // per
-    spot = np.arange(width)
-    slab = spot // LANES * per + spot % LANES // piece
-    order = np.zeros((width, width), np.float32)
-    order[spot, spot % piece * SLABS + slab] = 1.0
-    return pl.pallas_call(
-        merge_kernel,
-        out_shape=(jax.ShapeDtypeStruct((band, width), jnp.float32),
-                   jax.ShapeDtypeStruct((2, band, width), jnp.float32)),
-        compiler_params=pltpu.CompilerParams(vmem_limit_bytes=VMEM_BYTES),
-    )(records, jnp.asarray(order, jnp.bfloat16))
+        compiler_params=pltpu.CompilerParams(
+            collective_id=1, has_side_effects=True, vmem_limit_bytes=VMEM_BYTES),
+    )(smooth, power, pic, jnp.asarray(order, jnp.bfloat16))
 
 
 def shards(spectrum, plane_index, kernel_width, focus_gain):
@@ -362,18 +468,11 @@
     strip = row_transform(spectra, first, second, count)
     phase = line_phase(plane, jnp.arange(NX, dtype=jnp.int32))
     pic, power = column_transform(strip, jnp.stack([jnp.cos(phase), jnp.sin(phase)]))
-    band = power.shape[1]
-    forward = [(i, i + 1) for i in range(count - 1)]
-    backward = [(i + 1, i) for i in range(count - 1)]
-    low = lax.ppermute(power[:, band - 1:, :], "rows", forward)
-    high = lax.ppermute(power[:, :1, :], "rows", backward)
     inside = (jnp.arange(1, MAXWIDTH + 1) <= radius).astype(jnp.float32)
     smooth = jnp.concatenate([
         (2 * radius + 1).astype(jnp.float32)[None], inside, focus_gain,
         plane_index.astype(jnp.float32) / DEPTHS])[None]
-    records = score_records(smooth, power, low, high, pic, targets)
-    records = lax.all_to_all(records, "depth", split_axis=0, concat_axis=0, tiled=True)
-    return merge(records)
+    return focus(smooth, power, pic, targets, count)
 
 
 def solution(mesh):

time: 179 us -> 137 us (0.77); the launches traced: 177 us -> 136 us
  blocking collectives: 76.7 us -> 0 us
  Pallas kernels: 80.7 us -> 123 us
  starting transfers between devices: 5.55 us -> 0 us
    all_to_all x1 -> x0, blocking collectives: 76.7 us -> none  [shards(): lax.all_to_all(records, 'depth', split_axis=0, concat_axis=0, tiled=True)]
    pallas_call x2 -> x1, Pallas kernels: 16.6 us -> 58.4 us  [focus(): pl.pallas_call(partial(focus_kernel, groups, count), out_shape=(jax.Shape...]
    ppermute x2 -> x0, starting transfers between devices: 5.55 us -> none  [the longest x1 3.63 us: shards(): low = lax.ppermute(power[:, band - 1:, :], 'rows', forward)]
    unnamed x4 -> x2, local copies, waits for them, and re-layouts: 0.61 us -> 3.24 us
  transfers between devices with their start and end apart: 2 -> 0, of which waited for: 1 -> 0; matrix products, arithmetic and copies ran while one was open for 0% -> 0% of each run, Pallas kernels for 0% -> 0%
where the time goes in v2:
time: 137 us; the launch traced here: 136 us
  Pallas kernels  123 us (90%)
  other arithmetic  7.76 us (6%)
  local copies, waits for them, and re-layouts  3.51 us (3%)
  between operations  2.64 us (2%)
    pallas_call x1, Pallas kernels, focus(): pl.pallas_call(partial(focus_kernel, groups, count), out_shape=(jax.Shape...  58.4 us
    pallas_call x1, Pallas kernels, row_transform(): pl.pallas_call(partial(row_kernel, count, chunks), out_shape=jax.ShapeDty...  56.7 us
    pallas_call x1, Pallas kernels, column_transform(): pl.pallas_call(column_kernel, out_shape=(jax.ShapeDtypeStruct((2, SLABS,...  7.4 us
    unnamed x2, local copies, waits for them, and re-layouts  3.24 us
    convert_element_type x1, other arithmetic, row_table(): return (first.astype(jnp.bfloat16), (table - first).astype(jnp.bfloat16))  2.83 us

profile of v2, /device:TPU:11, one launch (start us, length us, event | category | flops | bytes accessed | tf_op | source)
XLA Modules:
  0.0 136.5 jit_solution(11133372131595502739)
XLA Ops:
  1.3 0.1 fusion.22
  1.4 0.1 fusion.27
  1.4 2.1 %fusion.29 = (f32[256,1024]{1,0:T(8,128)S(1)}, f32[256,1024]{1,0:T(8,128)S(1)}, f32[256,1024]{1,0:T(8,128)S(1)}) fusion(f32[256,1024]{1,0:T(8,128)} %constant.116.clone, f32[256,1024]{1,0:T(8,128)} %constant.115.clone, f32[1024]{0:T(1024)S(1)} %get-tuple-element.14, f32[256]{0:T(256)S(1)} %get-tuple-element.15, f32[1024]{0:T(1024)S(1)} %get-tuple-element.13, ...), kind=kLoop, calls=%fused_computation.69 | loop fusion | flops 3407872 | bytes 5253120 | tf_op jit(solution)/shard_map/neg | solution.py:49
  3.5 0.5 pad_maximum_fusion
  4.0 0.3 maximum_bitcast_fusion
  4.3 0.3 copy.11
  4.5 2.8 %fusion = (bf16[512,2048]{1,0:T(8,128)(2,1)}, bf16[512,2048]{1,0:T(8,128)(2,1)}) fusion(f32[2,2,2,64,2048]{4,3,2,1,0:T(8,128)S(1)} %copy.11), kind=kLoop, calls=%fused_computation.2 | loop fusion | flops 4194304 | bytes 8388608 | tf_op jit(solution)/shard_map/convert_element_type | solution.py:54
  7.4 56.7 %shard_map.104.strip_ref = f32[128,4096]{1,0:T(8,128)} custom-call(bf16[512,2048]{1,0:T(8,128)(2,1)} %get-tuple-element.7.first_ref, bf16[512,2048]{1,0:T(8,128)(2,1)} %get-tuple-element.6.second_ref, bf16[2048,4096]{1,0:T(8,128)(2,1)} %bitcast.17), custom_call_target="tpu_custom_call" | custom-call | tf_op jit(solution)/shard_map/pallas_call | solution.py:131
  64.1 0.7 fusion.9
  64.8 0.7 pad_maximum_fusion.2.phase_ref
  65.5 7.4 %shard_map.105 = (f32[2,32,64,128]{3,2,1,0:T(8,128)}, f32[32,64,128]{2,1,0:T(8,128)}) custom-call(f32[128,4096]{1,0:T(8,128)} %shard_map.104.strip_ref, f32[2,4096]{1,0:T(2,128)} %pad_maximum_fusion.2.phase_ref, f32[2,32,128]{2,1,0:T(8,128)} %constant.117.clone.twist_ref, f32[256,256]{1,0:T(8,128)} %constant.118.clone.table_ref), custom_call_target="tpu_custom_call" | custom-call | tf_op jit(solution)/shard_map/pallas_call | solution.py:215
  74.2 0.6 maximum_bitcast_fusion.1.smooth_ref
  74.8 58.4 %shard_map.106 = (f32[64,512]{1,0:T(8,128)}, f32[2,64,512]{2,1,0:T(8,128)}) custom-call(f32[1,6]{1,0:T(1,128)} %maximum_bitcast_fusion.1.smooth_ref, f32[32,64,128]{2,1,0:T(8,128)} %get-tuple-element.4.power_ref, f32[2,32,64,128]{3,2,1,0:T(8,128)} %get-tuple-element.5.pic_ref, bf16[512,512]{1,0:T(8,128)(2,1)} %constant.119.clone.order_ref), custom_call_target="tpu_custom_call" | custom-call | tf_op jit(solution)/shard_map/pallas_call | solution.py:440
  133.2 1.6 %copy.17 = f32[64,512]{1,0:T(8,128)} copy(f32[64,512]{1,0:T(8,128)} %get-tuple-element.21) | data formatting | bytes 262144
  134.8 1.7 %copy.18 = f32[2,64,512]{2,1,0:T(8,128)} copy(f32[2,64,512]{2,1,0:T(8,128)} %get-tuple-element.22) | data formatting | bytes 524288
  (1 shorter events, 0.0 us)

commit v3 on v2

v3 whole, which is shorter than its diff:
```python
from functools import partial
import math

import numpy as np
import jax
import jax.numpy as jnp
from jax import lax
from jax.experimental import pallas as pl
from jax.experimental.pallas import tpu as pltpu
from jax.sharding import PartitionSpec as P

NX = 4096
Y_WIN = 256
DEPTHS = 2048
MAXWIDTH = 3
LANES = 128
SLABS = NX // LANES
CORES = 2
UNIT = 1024
STRIP = 16
STEPS = 32767.0
TINY = 1e-33
VMEM_BYTES = 56 * 1024 * 1024


def line_phase(plane, freqs):
    signed = jnp.where(freqs < NX // 2, freqs, freqs - NX)
    square = signed * signed
    turns = (plane * (square % NX) + NX * (plane * (square // NX) % NX)) % (NX * NX)
    return turns.astype(jnp.float32) * (-2.0 * math.pi / (NX * NX))


def row_table(plane, place, count):
    freqs_n = NX // count
    band = Y_WIN // count
    turns = np.arange(Y_WIN)[:, None] * np.arange(freqs_n)[None, :] % NX
    angle = turns * (2.0 * np.pi / NX)
    base_cos = jnp.asarray(np.cos(angle).astype(np.float32))
    base_sin = jnp.asarray(np.sin(angle).astype(np.float32))
    phase = line_phase(plane, place * freqs_n + jnp.arange(freqs_n, dtype=jnp.int32))
    start = place * freqs_n * jnp.arange(Y_WIN, dtype=jnp.int32) % NX
    start_angle = start.astype(jnp.float32) * (2.0 * math.pi / NX)
    col_cos, col_sin = jnp.cos(phase)[None, :], jnp.sin(phase)[None, :]
    row_cos, row_sin = jnp.cos(start_angle)[:, None], jnp.sin(start_angle)[:, None]
    turn_cos = row_cos * col_cos - row_sin * col_sin
    turn_sin = row_cos * col_sin + row_sin * col_cos
    real = base_cos * turn_cos - base_sin * turn_sin
    imag = base_cos * turn_sin + base_sin * turn_cos
    upper = jnp.concatenate([real, -imag], axis=1)
    lower = jnp.concatenate([imag, real], axis=1)
    table = jnp.stack([upper, lower]).reshape(
        2, count // CORES, CORES, band // STRIP, STRIP, 2 * freqs_n)
    table = table.transpose(3, 2, 1, 0, 4, 5).reshape(band // STRIP, -1, 2 * freqs_n)
    first = lax.reduce_precision(table, 8, 7)
    return jnp.concatenate(
        [first.astype(jnp.bfloat16), (table - first).astype(jnp.bfloat16)], axis=1)


def butterflies(real, imag):
    n = len(real)
    if n == 1:
        return real, imag
    even_r, even_i = butterflies(real[0::2], imag[0::2])
    odd_r, odd_i = butterflies(real[1::2], imag[1::2])
    out_r, out_i = [None] * n, [None] * n
    for k in range(n // 2):
        c, s = math.cos(2.0 * math.pi * k / n), math.sin(2.0 * math.pi * k / n)
        if k == 0:
            tr, ti = odd_r[k], odd_i[k]
        elif 4 * k == n:
            tr, ti = -odd_i[k], odd_r[k]
        else:
            tr, ti = odd_r[k] * c - odd_i[k] * s, odd_r[k] * s + odd_i[k] * c
        out_r[k], out_i[k] = even_r[k] + tr, even_i[k] + ti
        out_r[k + n // 2], out_i[k + n // 2] = even_r[k] - tr, even_i[k] - ti
    return out_r, out_i


def wrapped(block, forward):
    lane = lax.broadcasted_iota(jnp.int32, block.shape, block.ndim - 1)
    shift = LANES - 1 if forward else 1
    edge = LANES - 1 if forward else 0
    return jnp.where(lane == edge, 0.0, pltpu.roll(block, shift, block.ndim - 1))


def kernel(count, smooth_ref, table_ref, phase_ref, twist_ref, dft_ref, order_ref, spec_ref,
           map_ref, field_ref, spec, part, core_in, half, chip_in, mid, pic, rim, energy, score,
           send_s, send_q, send_r, recv_s, recv_q, recv_r,
           loads, a_send, a_recv, b_send, b_recv, halo_send, halo_recv, sends, recvs):
    strips, targets, _, width = send_s.shape
    band = strips * STRIP
    groups = width // LANES
    piece = LANES // targets
    chips = count // CORES
    parts_n = NX // UNIT
    units = strips * parts_n
    half_rows = half.shape[1]
    block = 2 * STRIP
    place, me = lax.axis_index("rows"), lax.axis_index("depth")
    core, chip = lax.rem(place, CORES), lax.div(place, CORES)
    partner = chip * CORES + 1 - core
    has_low, has_high = place > 0, place < count - 1

    def load(c):
        return pltpu.make_async_copy(
            spec_ref.at[:, pl.ds(c * UNIT, UNIT)], spec.at[c], loads.at[c])

    def other(hop):
        return lax.rem(chip + hop, chips)

    def remote(src, dst, send, recv, target):
        return pltpu.make_async_remote_copy(
            src_ref=src, dst_ref=dst, send_sem=send, recv_sem=recv,
            device_id=target, device_id_type=pl.DeviceIdType.MESH)

    def core_copy(u):
        rows = pl.ds(pl.multiple_of((1 - core) * half_rows, half_rows), half_rows)
        return remote(part.at[u, rows], core_in.at[u], a_send.at[u], a_recv.at[u],
                      {"rows": partner})

    def chip_copy(u, hop):
        rows = pl.ds(pl.multiple_of(other(hop) * block, block), block)
        return remote(half.at[u, rows], chip_in.at[u, hop - 1], b_send.at[u, hop - 1],
                      b_recv.at[u, hop - 1], {"rows": other(hop) * CORES + core})

    def halo(kind):
        low = kind == 0
        own = pl.ds(8 if low else band, 8)
        there = pl.ds(8 + band if low else 0, 8)
        return remote(rim.at[pl.ds(1, SLABS), own], rim.at[pl.ds(1, SLABS), there],
                      halo_send.at[kind], halo_recv.at[kind],
                      {"rows": lax.rem(place + (count - 1 if low else 1), count)})

    def copies(s, hop):
        target = lax.rem(me + hop, targets)
        return [remote(src.at[s, target], dst.at[s, hop - 1], sends.at[s, hop - 1, i],
                       recvs.at[s, hop - 1, i], {"depth": target})
                for i, (src, dst) in enumerate(
                    ((send_s, recv_s), (send_q, recv_q), (send_r, recv_r)))]

    for c in range(parts_n):
        load(c).start()

    barrier = pltpu.get_barrier_semaphore()

    def greet(target):
        pl.semaphore_signal(barrier, inc=1, device_id=target,
                            device_id_type=pl.DeviceIdType.MESH)

    greet({"rows": partner})
    for hop in range(1, chips):
        greet({"rows": other(hop) * CORES + core})

    @pl.when(has_low)
    def _():
        greet({"rows": place - 1})

    @pl.when(has_high)
    def _():
        greet({"rows": place + 1})

    @pl.loop(1, targets)
    def _(hop):
        greet({"depth": lax.rem(me + hop, targets)})

    pl.semaphore_wait(barrier, chips + targets - 1 + has_low.astype(jnp.int32)
                      + has_high.astype(jnp.int32))

    @pl.when(place == 0)
    def _():
        rim[1:SLABS + 1, 0:8, :] = jnp.zeros((SLABS, 8, LANES), jnp.float32)

    @pl.when(place == count - 1)
    def _():
        rim[1:SLABS + 1, 8 + band:16 + band, :] = jnp.zeros((SLABS, 8, LANES), jnp.float32)

    def pass_on(u):
        core_copy(u).wait()
        rows = pl.ds(pl.multiple_of(core * half_rows, half_rows), half_rows)
        half[u] = part[u, rows] + core_in[u]
        for hop in range(1, chips):
            chip_copy(u, hop).start()

    @pl.loop(0, units)
    def _(u):
        strip, c = u // parts_n, u % parts_n

        @pl.when(u < parts_n)
        def _():
            load(u).wait()

        both = jnp.dot(table_ref[strip], spec[c], preferred_element_type=jnp.float32)
        part[u] = both[:CORES * half_rows] + both[CORES * half_rows:]
        core_copy(u).start()

        @pl.when(u >= 1)
        def _():
            pass_on(u - 1)

    pass_on(units - 1)

    def columns(k):
        for c in range(parts_n):
            for hop in range(1, chips):
                chip_copy(k * parts_n + c, hop).wait()

        @pl.loop(0, STRIP // 8)
        def _(s):
            at = pl.multiple_of(s * 8, 8)
            base = pl.multiple_of(chip * block + at, 8)
            real, imag = [], []
            for slab in range(SLABS):
                u = k * parts_n + slab * LANES // UNIT
                inner = slab * LANES % UNIT
                lanes = slice(inner, inner + LANES)

                def total(offset):
                    value = half[u, pl.ds(base + offset, 8), lanes]
                    for hop in range(1, chips):
                        value = value + chip_in[u, hop - 1, pl.ds(at + offset, 8), lanes]
                    return value

                xr, xi = total(0), total(STRIP)
                lanes = slice(slab * LANES, (slab + 1) * LANES)
                pc, ps = phase_ref[0:1, lanes], phase_ref[1:2, lanes]
                real.append(xr * pc - xi * ps)
                imag.append(xr * ps + xi * pc)
            real, imag = butterflies(real, imag)
            for slab in range(SLABS):
                tc, ts = twist_ref[0, slab:slab + 1, :], twist_ref[1, slab:slab + 1, :]
                mid[slab, pl.ds(at, 8), 0:LANES] = real[slab] * tc - imag[slab] * ts
                mid[slab, pl.ds(at, 8), LANES:2 * LANES] = real[slab] * ts + imag[slab] * tc

        per = 16
        at = pl.multiple_of(k * STRIP, STRIP)

        @pl.loop(0, SLABS // per)
        def _(q):
            slabs = pl.ds(q * per, per)
            rows = mid[slabs].reshape(per * STRIP, 2 * LANES)
            both = jnp.dot(rows, dft_ref[...], precision=lax.Precision.HIGHEST,
                           preferred_element_type=jnp.float32)
            real, imag = both[:, :LANES], both[:, LANES:]
            pic[0, slabs, pl.ds(at, STRIP)] = real.reshape(per, STRIP, LANES)
            pic[1, slabs, pl.ds(at, STRIP)] = imag.reshape(per, STRIP, LANES)
            rim[pl.ds(q * per + 1, per), pl.ds(at + 8, STRIP)] = (
                real * real + imag * imag).reshape(per, STRIP, LANES)

    def rows_of(g):
        return [pl.multiple_of(lax.rem(g * STRIP + band - 8, band), 8),
                pl.multiple_of(g * STRIP, 8)]

    def records(g):
        runs = rows_of(g)
        for n, run in enumerate(runs):
            window = pl.ds(run, 24)
            out = slice(8 * n, 8 * n + 8)
            rim[0, window, :] = wrapped(rim[SLABS, window, :], False)
            rim[SLABS + 1, window, :] = wrapped(rim[1, window, :], True)

            @pl.loop(0, SLABS)
            def _(slab):
                before, here, after = (rim[slab + j, window, :] for j in range(3))

                def vertical(x):
                    return x[7:15] + 2.0 * x[8:16] + x[9:17]

                across = vertical(after) - vertical(before)
                horizontal = before + 2.0 * here + after
                downward = horizontal[9:17] - horizontal[7:15]
                energy[slab + MAXWIDTH, out, :] = across * across + downward * downward

        for k in range(MAXWIDTH):
            energy[k] = wrapped(energy[SLABS + k], False)
            energy[SLABS + MAXWIDTH + k] = wrapped(energy[MAXWIDTH + k], True)

        @pl.loop(0, SLABS)
        def _(slab):
            total = energy[slab + MAXWIDTH]
            for k in range(1, MAXWIDTH + 1):
                total = total + smooth_ref[0, k] * (
                    energy[slab + MAXWIDTH - k] + energy[slab + MAXWIDTH + k])
            score[slab] = smooth_ref[0, 4] * jnp.log(1.0 + total / smooth_ref[0, 0])

        block_of = lax.broadcasted_iota(jnp.int32, (STRIP, LANES), 1) // piece

        def exchanged(held):
            gap = 1
            while gap < targets:
                low_lane = block_of // gap % 2 == 0
                for i in range(targets):
                    if i // gap % 2 == 0:
                        a, c = held[i], held[i + gap]
                        held[i] = jnp.where(low_lane, a, pltpu.roll(c, gap * piece, 1))
                        held[i + gap] = jnp.where(
                            low_lane, pltpu.roll(a, LANES - gap * piece, 1), c)
                gap *= 2
            return held

        @pl.loop(0, groups)
        def _(q):
            lanes = pl.ds(pl.multiple_of(q * LANES, LANES), LANES)
            held = exchanged([score[q * targets + i] for i in range(targets)])
            for d in range(targets):
                send_s[g, d, :, lanes] = held[d]
            real, imag = (
                exchanged([
                    jnp.concatenate([pic[kind, q * targets + i, pl.ds(run, 8), :]
                                     for run in runs], axis=0)
                    for i in range(targets)])
                for kind in range(2))
            for d in range(targets):
                largest = jnp.max(jnp.maximum(jnp.abs(real[d]), jnp.abs(imag[d])),
                                  axis=0, keepdims=True)
                largest = jnp.maximum(largest, TINY)
                send_r[g, d, :, lanes] = largest * (1.0 / STEPS)
                scale = STEPS / largest
                for kind, value in ((0, real[d]), (1, imag[d])):
                    level = jnp.floor(value * scale + 0.5).astype(jnp.int32)
                    send_q[g, d, kind * STRIP:(kind + 1) * STRIP, lanes] = level.astype(jnp.int16)

        for d in range(targets):
            send_r[g, d, :, width:width + LANES] = jnp.full((1, LANES), smooth_ref[0, 5])

        @pl.loop(1, targets)
        def _(hop):
            for copy in copies(g, hop):
                copy.start()

        recv_s[g, targets - 1] = send_s[g, me]
        recv_q[g, targets - 1] = send_q[g, me]
        recv_r[g, targets - 1] = send_r[g, me]

    @pl.loop(0, strips)
    def _(k):
        columns(k)

        @pl.when(jnp.logical_and(k == 0, has_low))
        def _():
            halo(0).start()

        @pl.when(jnp.logical_and(k == strips - 1, has_high))
        def _():
            halo(1).start()

        @pl.when(k == strips - 1)
        def _():
            @pl.when(has_low)
            def _():
                halo(0).wait_send()

            @pl.when(has_high)
            def _():
                halo(0).wait_recv()

        @pl.when(k >= 1)
        def _():
            records(k)

    @pl.when(has_high)
    def _():
        halo(1).wait_send()

    @pl.when(has_low)
    def _():
        halo(1).wait_recv()

    records(0)

    @pl.loop(0, strips)
    def _(turn):
        g = lax.rem(turn + 1, strips)

        @pl.loop(1, targets)
        def _(hop):
            for copy in copies(g, hop):
                copy.wait()

        peak = recv_s[g, 0]
        for p in range(1, targets):
            peak = jnp.maximum(peak, recv_s[g, p])
        summed = jnp.zeros_like(peak)
        totals = [jnp.zeros_like(peak) for _ in range(3)]
        for p in range(targets):
            weight = jnp.exp(recv_s[g, p] - peak)
            summed = summed + weight
            totals[0] = totals[0] + weight * recv_r[g, p, :, width:width + 1]
            scaled = weight * recv_r[g, p, :, 0:width]
            for kind in range(2):
                level = recv_q[g, p, kind * STRIP:(kind + 1) * STRIP, :]
                totals[1 + kind] = totals[1 + kind] + scaled * level.astype(jnp.int32).astype(
                    jnp.float32)
        merged = jnp.concatenate([total / summed for total in totals], axis=0)
        placed = jnp.zeros_like(merged)
        for _ in range(3):
            term = merged.astype(jnp.bfloat16)
            placed = placed + jnp.dot(term, order_ref[...], preferred_element_type=jnp.float32)
            merged = merged - term.astype(jnp.float32)
        for n, run in enumerate(rows_of(g)):
            rows = pl.ds(run, 8)
            map_ref[rows, :] = placed[8 * n:8 * n + 8]
            field_ref[0, rows, :] = placed[STRIP + 8 * n:STRIP + 8 * n + 8]
            field_ref[1, rows, :] = placed[2 * STRIP + 8 * n:2 * STRIP + 8 * n + 8]


def refocus(smooth, table, phase, spectra, count, targets):
    band = Y_WIN // count
    strips = band // STRIP
    groups = SLABS // targets
    width = groups * LANES
    piece = LANES // targets
    chips = count // CORES
    units = strips * NX // UNIT
    half_rows = chips * 2 * STRIP
    lane = np.arange(LANES)
    twist = np.arange(SLABS)[:, None] * lane[None, :] * (2.0 * np.pi / NX)
    twist = np.stack([np.cos(twist), np.sin(twist)]).astype(np.float32)
    angle = lane[:, None] * lane[None, :] % LANES * (2.0 * np.pi / LANES)
    cosine, sine = np.cos(angle) / NX, np.sin(angle) / NX
    dft = np.block([[cosine, sine], [-sine, cosine]]).astype(np.float32)
    spot = np.arange(width)
    slab = spot // LANES * targets + spot % LANES // piece
    order = np.zeros((width, width), np.float32)
    order[spot, spot % piece * SLABS + slab] = 1.0
    vmem = pl.BlockSpec(memory_space=pltpu.VMEM)
    records = [
        pltpu.VMEM((strips, targets, STRIP, width), jnp.float32),
        pltpu.VMEM((strips, targets, 2 * STRIP, width), jnp.int16),
        pltpu.VMEM((strips, targets, 1, width + LANES), jnp.float32),
    ]
    return pl.pallas_call(
        partial(kernel, count),
        out_shape=(jax.ShapeDtypeStruct((band, width), jnp.float32),
                   jax.ShapeDtypeStruct((2, band, width), jnp.float32)),
        in_specs=[pl.BlockSpec(memory_space=pltpu.SMEM)] + [vmem] * 5
        + [pl.BlockSpec(memory_space=pl.ANY)],
        out_specs=(vmem, vmem),
        scratch_shapes=[
            pltpu.VMEM((NX // UNIT, spectra.shape[0], UNIT), jnp.bfloat16),
            pltpu.VMEM((units, CORES * half_rows, UNIT), jnp.float32),
            pltpu.VMEM((units, half_rows, UNIT), jnp.float32),
            pltpu.VMEM((units, half_rows, UNIT), jnp.float32),
            pltpu.VMEM((units, chips - 1, 2 * STRIP, UNIT), jnp.float32),
            pltpu.VMEM((SLABS, STRIP, 2 * LANES), jnp.float32),
            pltpu.VMEM((2, SLABS, band, LANES), jnp.float32),
            pltpu.VMEM((SLABS + 2, band + 16, LANES), jnp.float32),
            pltpu.VMEM((SLABS + 2 * MAXWIDTH, STRIP, LANES), jnp.float32),
            pltpu.VMEM((SLABS, STRIP, LANES), jnp.float32),
            *records, *records,
            pltpu.SemaphoreType.DMA((NX // UNIT,)),
            pltpu.SemaphoreType.DMA((units,)),
            pltpu.SemaphoreType.DMA((units,)),
            pltpu.SemaphoreType.DMA((units, chips - 1)),
            pltpu.SemaphoreType.DMA((units, chips - 1)),
            pltpu.SemaphoreType.DMA((2,)),
            pltpu.SemaphoreType.DMA((2,)),
            pltpu.SemaphoreType.DMA((strips, targets - 1, 3)),
            pltpu.SemaphoreType.DMA((strips, targets - 1, 3)),
        ],
        compiler_params=pltpu.CompilerParams(
            collective_id=0, has_side_effects=True, vmem_limit_bytes=VMEM_BYTES),
    )(smooth, table, phase, jnp.asarray(twist), jnp.asarray(dft),
      jnp.asarray(order, jnp.bfloat16), spectra)


def shards(spectrum, plane_index, kernel_width, focus_gain):
    count = lax.axis_size("rows")
    targets = lax.axis_size("depth")
    place = lax.axis_index("rows")
    plane, radius = plane_index[0], kernel_width[0]
    table = row_table(plane, place, count)
    spectra = spectrum.reshape(2 * spectrum.shape[1], NX)
    phase = line_phase(plane, jnp.arange(NX, dtype=jnp.int32))
    phase = jnp.stack([jnp.cos(phase), jnp.sin(phase)])
    inside = (jnp.arange(1, MAXWIDTH + 1) <= radius).astype(jnp.float32)
    smooth = jnp.concatenate([
        (2 * radius + 1).astype(jnp.float32)[None], inside, focus_gain,
        plane_index.astype(jnp.float32) / DEPTHS])[None]
    return refocus(smooth, table, phase, spectra, count, targets)


def solution(mesh):
    return jax.shard_map(
        shards,
        mesh=mesh,
        in_specs=(P(None, "rows", None), P("depth"), P("depth"), P("depth")),
        out_specs=(P("rows", "depth"), P(None, "rows", "depth")),
        check_vma=False,
    )
```

time: 137 us -> 104 us (0.76)
  Pallas kernels: 123 us -> 89.1 us
    pallas_call x3 -> x1, Pallas kernels: 123 us -> 89.1 us  [refocus(): pl.pallas_call(partial(kernel, count), out_shape=(jax.ShapeDtypeStruct((b...]
    concatenate x0 -> x1, other arithmetic: none -> 2.53 us  [row_table(): jnp.concatenate([first.astype(jnp.bfloat16), (table - first).astype(jnp.b...]
    convert_element_type x1, other arithmetic: 2.83 us -> 0.84 us  [row_table(): first.astype(jnp.bfloat16)]
where the time goes in v3:
time: 104 us
  Pallas kernels  89.1 us (86%)
  other arithmetic  8.29 us (8%)
  local copies, waits for them, and re-layouts  3.51 us (3%)
  between operations  2.64 us (3%)
    pallas_call x1, Pallas kernels, refocus(): pl.pallas_call(partial(kernel, count), out_shape=(jax.ShapeDtypeStruct((b...  89.1 us
    unnamed x2, local copies, waits for them, and re-layouts  3.24 us
    concatenate x1, other arithmetic, row_table(): jnp.concatenate([first.astype(jnp.bfloat16), (table - first).astype(jnp.b...  2.53 us

profile of v3, /device:TPU:11, one launch (start us, length us, event | category | flops | bytes accessed | tf_op | source)
XLA Modules:
  0.0 103.5 jit_solution(4662120675986170693)
XLA Ops:
  1.3 0.1 fusion.22
  1.4 0.1 fusion.27
  1.4 2.1 %fusion.29 = (f32[256,1024]{1,0:T(8,128)S(1)}, f32[256,1024]{1,0:T(8,128)S(1)}, f32[256,1024]{1,0:T(8,128)S(1)}) fusion(f32[256,1024]{1,0:T(8,128)} %constant.116.clone, f32[256,1024]{1,0:T(8,128)} %constant.115.clone, f32[1024]{0:T(1024)S(1)} %get-tuple-element.10, f32[256]{0:T(256)S(1)} %get-tuple-element.11, f32[1024]{0:T(1024)S(1)} %get-tuple-element.9, ...), kind=kLoop, calls=%fused_computation.70 | loop fusion | flops 3407872 | bytes 5253120 | tf_op jit(solution)/shard_map/neg | solution.py:49
  3.5 0.5 pad_maximum_fusion.1
  4.0 0.3 maximum_bitcast_fusion
  4.3 0.3 copy.11
  4.5 0.8 reduce-precision_convert_fusion
  5.4 2.5 %pad_maximum_fusion.table_ref = bf16[4,256,2048]{2,1,0:T(8,128)(2,1)} fusion(bf16[4,128,2048]{2,1,0:T(8,128)(2,1)S(1)} %get-tuple-element.3, bf16[4,128,2048]{2,1,0:T(8,128)(2,1)S(1)} %get-tuple-element.2), kind=kLoop, calls=%fused_computation.4 | loop fusion | flops 8388608 | bytes 8388608 | tf_op jit(solution)/shard_map/concatenate | solution.py:55
  7.9 0.7 fusion.9
  8.6 0.7 pad_maximum_fusion.3.phase_ref
  10.6 0.6 maximum_bitcast_fusion.1.smooth_ref
  11.2 89.1 %shard_map.104 = (f32[64,512]{1,0:T(8,128)}, f32[2,64,512]{2,1,0:T(8,128)}) custom-call(f32[1,6]{1,0:T(1,128)} %maximum_bitcast_fusion.1.smooth_ref, bf16[4,256,2048]{2,1,0:T(8,128)(2,1)} %pad_maximum_fusion.table_ref, f32[2,4096]{1,0:T(2,128)} %pad_maximum_fusion.3.phase_ref, f32[2,32,128]{2,1,0:T(8,128)} %constant.117.clone.twist_ref, ...), custom_call_target="tpu_custom_call" | custom-call | tf_op jit(solution)/shard_map/pallas_call | solution.py:431
  100.3 1.6 %copy.17 = f32[64,512]{1,0:T(8,128)} copy(f32[64,512]{1,0:T(8,128)} %get-tuple-element.17) | data formatting | bytes 262144
  101.8 1.7 %copy.18 = f32[2,64,512]{2,1,0:T(8,128)} copy(f32[2,64,512]{2,1,0:T(8,128)} %get-tuple-element.18) | data formatting | bytes 524288
  (1 shorter events, 0.0 us)

commit v4 on v3

--- a/solution.py
+++ b/solution.py
@@ -20,6 +20,8 @@
 STRIP = 16
 STEPS = 32767.0
 TINY = 1e-33
+FINE_STEPS = 8388000.0
+FINE_TINY = 1e-30
 VMEM_BYTES = 56 * 1024 * 1024
 
 
@@ -76,6 +78,23 @@
     return out_r, out_i
 
 
+def fine_code(value):
+    largest = jnp.max(jnp.abs(value), axis=0, keepdims=True)
+    largest = jnp.maximum(largest, FINE_TINY)
+    level = jnp.floor(value * (FINE_STEPS / largest) + 0.5).astype(jnp.int32)
+    upper = (level + 128) >> 8
+    rest = level - (upper << 8)
+    packed = jnp.maximum(rest[:STRIP], -127) * 256 + rest[STRIP:]
+    return upper.astype(jnp.int16), packed.astype(jnp.int16), largest * (1.0 / FINE_STEPS)
+
+
+def fine_value(upper, packed, unit):
+    packed = packed.astype(jnp.int32)
+    second = ((packed + 128) & 255) - 128
+    rest = jnp.concatenate([(packed - second) >> 8, second], axis=0)
+    return (upper.astype(jnp.int32) * 256 + rest).astype(jnp.float32) * unit
+
+
 def wrapped(block, forward):
     lane = lax.broadcasted_iota(jnp.int32, block.shape, block.ndim - 1)
     shift = LANES - 1 if forward else 1
@@ -84,7 +103,8 @@
 
 
 def kernel(count, smooth_ref, table_ref, phase_ref, twist_ref, dft_ref, order_ref, spec_ref,
-           map_ref, field_ref, spec, part, core_in, half, chip_in, mid, pic, rim, energy, score,
+           map_ref, field_ref, spec, part, core_in, half,
+           code_out, unit_out, code_in, unit_in, strip_sum, mid, pic, rim, energy, score,
            send_s, send_q, send_r, recv_s, recv_q, recv_r,
            loads, a_send, a_recv, b_send, b_recv, halo_send, halo_recv, sends, recvs):
     strips, targets, _, width = send_s.shape
@@ -118,10 +138,10 @@
         return remote(part.at[u, rows], core_in.at[u], a_send.at[u], a_recv.at[u],
                       {"rows": partner})
 
-    def chip_copy(u, hop):
-        rows = pl.ds(pl.multiple_of(other(hop) * block, block), block)
-        return remote(half.at[u, rows], chip_in.at[u, hop - 1], b_send.at[u, hop - 1],
-                      b_recv.at[u, hop - 1], {"rows": other(hop) * CORES + core})
+    def chip_copies(u, hop):
+        return [remote(src.at[u, hop - 1], dst.at[u, hop - 1], b_send.at[u, hop - 1, i],
+                       b_recv.at[u, hop - 1, i], {"rows": other(hop) * CORES + core})
+                for i, (src, dst) in enumerate(((code_out, code_in), (unit_out, unit_in)))]
 
     def halo(kind):
         low = kind == 0
@@ -179,7 +199,13 @@
         rows = pl.ds(pl.multiple_of(core * half_rows, half_rows), half_rows)
         half[u] = part[u, rows] + core_in[u]
         for hop in range(1, chips):
-            chip_copy(u, hop).start()
+            rows = pl.ds(pl.multiple_of(other(hop) * block, block), block)
+            upper, packed, unit = fine_code(half[u, rows])
+            code_out[u, hop - 1, 0:block, :] = upper
+            code_out[u, hop - 1, block:block + STRIP, :] = packed
+            unit_out[u, hop - 1] = unit
+            for copy in chip_copies(u, hop):
+                copy.start()
 
     @pl.loop(0, units)
     def _(u):
@@ -200,28 +226,26 @@
     pass_on(units - 1)
 
     def columns(k):
+        rows = pl.ds(pl.multiple_of(chip * block, block), block)
         for c in range(parts_n):
+            u = k * parts_n + c
+            total = half[u, rows]
             for hop in range(1, chips):
-                chip_copy(k * parts_n + c, hop).wait()
+                for copy in chip_copies(u, hop):
+                    copy.wait()
+                total = total + fine_value(
+                    code_in[u, hop - 1, 0:block, :], code_in[u, hop - 1, block:block + STRIP, :],
+                    unit_in[u, hop - 1])
+            strip_sum[:, c * UNIT:(c + 1) * UNIT] = total
 
         @pl.loop(0, STRIP // 8)
         def _(s):
             at = pl.multiple_of(s * 8, 8)
-            base = pl.multiple_of(chip * block + at, 8)
             real, imag = [], []
             for slab in range(SLABS):
-                u = k * parts_n + slab * LANES // UNIT
-                inner = slab * LANES % UNIT
-                lanes = slice(inner, inner + LANES)
-
-                def total(offset):
-                    value = half[u, pl.ds(base + offset, 8), lanes]
-                    for hop in range(1, chips):
-                        value = value + chip_in[u, hop - 1, pl.ds(at + offset, 8), lanes]
-                    return value
-
-                xr, xi = total(0), total(STRIP)
                 lanes = slice(slab * LANES, (slab + 1) * LANES)
+                xr = strip_sum[pl.ds(at, 8), lanes]
+                xi = strip_sum[pl.ds(STRIP + at, 8), lanes]
                 pc, ps = phase_ref[0:1, lanes], phase_ref[1:2, lanes]
                 real.append(xr * pc - xi * ps)
                 imag.append(xr * ps + xi * pc)
@@ -423,6 +447,10 @@
     order = np.zeros((width, width), np.float32)
     order[spot, spot % piece * SLABS + slab] = 1.0
     vmem = pl.BlockSpec(memory_space=pltpu.VMEM)
+    codes = [
+        pltpu.VMEM((units, chips - 1, 3 * STRIP, UNIT), jnp.int16),
+        pltpu.VMEM((units, chips - 1, 1, UNIT), jnp.float32),
+    ]
     records = [
         pltpu.VMEM((strips, targets, STRIP, width), jnp.float32),
         pltpu.VMEM((strips, targets, 2 * STRIP, width), jnp.int16),
@@ -440,7 +468,8 @@
             pltpu.VMEM((units, CORES * half_rows, UNIT), jnp.float32),
             pltpu.VMEM((units, half_rows, UNIT), jnp.float32),
             pltpu.VMEM((units, half_rows, UNIT), jnp.float32),
-            pltpu.VMEM((units, chips - 1, 2 * STRIP, UNIT), jnp.float32),
+            *codes, *codes,
+            pltpu.VMEM((2 * STRIP, NX), jnp.float32),
             pltpu.VMEM((SLABS, STRIP, 2 * LANES), jnp.float32),
             pltpu.VMEM((2, SLABS, band, LANES), jnp.float32),
             pltpu.VMEM((SLABS + 2, band + 16, LANES), jnp.float32),
@@ -450,8 +479,8 @@
             pltpu.SemaphoreType.DMA((NX // UNIT,)),
             pltpu.SemaphoreType.DMA((units,)),
             pltpu.SemaphoreType.DMA((units,)),
-            pltpu.SemaphoreType.DMA((units, chips - 1)),
-            pltpu.SemaphoreType.DMA((units, chips - 1)),
+            pltpu.SemaphoreType.DMA((units, chips - 1, 2)),
+            pltpu.SemaphoreType.DMA((units, chips - 1, 2)),
             pltpu.SemaphoreType.DMA((2,)),
             pltpu.SemaphoreType.DMA((2,)),
             pltpu.SemaphoreType.DMA((strips, targets - 1, 3)),

time: 104 us -> 101 us (0.971)
  Pallas kernels: 89.1 us -> 86.7 us
    pallas_call x1, Pallas kernels: 89.1 us -> 86.7 us  [refocus(): pl.pallas_call(partial(kernel, count), out_shape=(jax.ShapeDtypeStruct((b...]
where the time goes in v4:
time: 101 us
  Pallas kernels  86.7 us (86%)
  other arithmetic  8.29 us (8%)
  local copies, waits for them, and re-layouts  3.51 us (3%)
  between operations  2.64 us (3%)
    pallas_call x1, Pallas kernels, refocus(): pl.pallas_call(partial(kernel, count), out_shape=(jax.ShapeDtypeStruct((b...  86.7 us
    unnamed x2, local copies, waits for them, and re-layouts  3.24 us
    concatenate x1, other arithmetic, row_table(): jnp.concatenate([first.astype(jnp.bfloat16), (table - first).astype(jnp.b...  2.53 us
    neg x1, other arithmetic, row_table(): upper = jnp.concatenate([real, -imag], axis=1)  2.07 us

profile of v4, /device:TPU:11, one launch (start us, length us, event | category | flops | bytes accessed | tf_op | source)
XLA Modules:
  0.0 101.2 jit_solution(5265054201196923966)
XLA Ops:
  1.3 0.1 fusion.22
  1.4 0.1 fusion.27
  1.4 2.1 %fusion.29 = (f32[256,1024]{1,0:T(8,128)S(1)}, f32[256,1024]{1,0:T(8,128)S(1)}, f32[256,1024]{1,0:T(8,128)S(1)}) fusion(f32[256,1024]{1,0:T(8,128)} %constant.116.clone, f32[256,1024]{1,0:T(8,128)} %constant.115.clone, f32[1024]{0:T(1024)S(1)} %get-tuple-element.10, f32[256]{0:T(256)S(1)} %get-tuple-element.11, f32[1024]{0:T(1024)S(1)} %get-tuple-element.9, ...), kind=kLoop, calls=%fused_computation.70 | loop fusion | flops 3407872 | bytes 5253120 | tf_op jit(solution)/shard_map/neg | solution.py:51
  3.5 0.5 pad_maximum_fusion.1
  4.0 0.3 maximum_bitcast_fusion
  4.3 0.3 copy.11
  4.5 0.8 reduce-precision_convert_fusion
  5.4 2.5 %pad_maximum_fusion.table_ref = bf16[4,256,2048]{2,1,0:T(8,128)(2,1)} fusion(bf16[4,128,2048]{2,1,0:T(8,128)(2,1)S(1)} %get-tuple-element.3, bf16[4,128,2048]{2,1,0:T(8,128)(2,1)S(1)} %get-tuple-element.2), kind=kLoop, calls=%fused_computation.4 | loop fusion | flops 8388608 | bytes 8388608 | tf_op jit(solution)/shard_map/concatenate | solution.py:57
  7.9 0.7 fusion.9
  8.6 0.7 pad_maximum_fusion.3.phase_ref
  10.6 0.6 maximum_bitcast_fusion.1.smooth_ref
  11.2 86.7 %shard_map.104 = (f32[64,512]{1,0:T(8,128)}, f32[2,64,512]{2,1,0:T(8,128)}) custom-call(f32[1,6]{1,0:T(1,128)} %maximum_bitcast_fusion.1.smooth_ref, bf16[4,256,2048]{2,1,0:T(8,128)(2,1)} %pad_maximum_fusion.table_ref, f32[2,4096]{1,0:T(2,128)} %pad_maximum_fusion.3.phase_ref, f32[2,32,128]{2,1,0:T(8,128)} %constant.117.clone.twist_ref, ...), custom_call_target="tpu_custom_call" | custom-call | tf_op jit(solution)/shard_map/pallas_call | solution.py:459
  97.9 1.6 %copy.17 = f32[64,512]{1,0:T(8,128)} copy(f32[64,512]{1,0:T(8,128)} %get-tuple-element.17) | data formatting | bytes 262144
  99.5 1.7 %copy.18 = f32[2,64,512]{2,1,0:T(8,128)} copy(f32[2,64,512]{2,1,0:T(8,128)} %get-tuple-element.18) | data formatting | bytes 524288
  (1 shorter events, 0.0 us)

commit v5 on v4

--- a/solution.py
+++ b/solution.py
@@ -30,6 +30,10 @@
     square = signed * signed
     turns = (plane * (square % NX) + NX * (plane * (square // NX) % NX)) % (NX * NX)
     return turns.astype(jnp.float32) * (-2.0 * math.pi / (NX * NX))
+
+
+def pair_of(band):
+    return 2 if band // STRIP % 2 == 0 else 1
 
 
 def row_table(plane, place, count):
@@ -52,7 +56,8 @@
     lower = jnp.concatenate([imag, real], axis=1)
     table = jnp.stack([upper, lower]).reshape(
         2, count // CORES, CORES, band // STRIP, STRIP, 2 * freqs_n)
-    table = table.transpose(3, 2, 1, 0, 4, 5).reshape(band // STRIP, -1, 2 * freqs_n)
+    table = table.transpose(3, 2, 1, 0, 4, 5)
+    table = table.reshape(band // STRIP // pair_of(band), -1, 2 * freqs_n)
     first = lax.reduce_precision(table, 8, 7)
     return jnp.concatenate(
         [first.astype(jnp.bfloat16), (table - first).astype(jnp.bfloat16)], axis=1)
@@ -207,23 +212,35 @@
             for copy in chip_copies(u, hop):
                 copy.start()
 
-    @pl.loop(0, units)
-    def _(u):
-        strip, c = u // parts_n, u % parts_n
-
-        @pl.when(u < parts_n)
-        def _():
-            load(u).wait()
-
-        both = jnp.dot(table_ref[strip], spec[c], preferred_element_type=jnp.float32)
-        part[u] = both[:CORES * half_rows] + both[CORES * half_rows:]
-        core_copy(u).start()
-
-        @pl.when(u >= 1)
-        def _():
-            pass_on(u - 1)
-
-    pass_on(units - 1)
+    pair = pair_of(band)
+    part_rows = CORES * half_rows
+
+    def unit_of(p, c, i):
+        return (p * pair + i) * parts_n + c
+
+    def pass_all(p, c):
+        for i in range(pair):
+            pass_on(unit_of(p, c, i))
+
+    def rows_transform(p):
+        @pl.loop(0, parts_n)
+        def _(c):
+            @pl.when(p == 0)
+            def _():
+                load(c).wait()
+
+            both = jnp.dot(table_ref[p], spec[c], preferred_element_type=jnp.float32)
+            for i in range(pair):
+                u = unit_of(p, c, i)
+                low, high = i * part_rows, (pair + i) * part_rows
+                part[u] = both[low:low + part_rows] + both[high:high + part_rows]
+                core_copy(u).start()
+
+            @pl.when(c >= 1)
+            def _():
+                pass_all(p, c - 1)
+
+        pass_all(p, parts_n - 1)
 
     def columns(k):
         rows = pl.ds(pl.multiple_of(chip * block, block), block)
@@ -357,6 +374,10 @@
 
     @pl.loop(0, strips)
     def _(k):
+        @pl.when(k % pair == 0)
+        def _():
+            rows_transform(k // pair)
+
         columns(k)
 
         @pl.when(jnp.logical_and(k == 0, has_low))
@@ -367,19 +388,17 @@
         def _():
             halo(1).start()
 
-        @pl.when(k == strips - 1)
-        def _():
-            @pl.when(has_low)
-            def _():
-                halo(0).wait_send()
-
-            @pl.when(has_high)
-            def _():
-                halo(0).wait_recv()
-
         @pl.when(k >= 1)
         def _():
             records(k)
+
+    @pl.when(has_low)
+    def _():
+        halo(0).wait_send()
+
+    @pl.when(has_high)
+    def _():
+        halo(0).wait_recv()
 
     @pl.when(has_high)
     def _():

time: 101 us -> 113 us (1.12); the launches traced: 101 us -> 112 us
  Pallas kernels: 86.7 us -> 97.2 us
    pallas_call x1, Pallas kernels: 86.7 us -> 97.2 us  [refocus(): pl.pallas_call(partial(kernel, count), out_shape=(jax.ShapeDtypeStruct((b...]
where the time goes in v5:
time: 113 us; the launch traced here: 112 us
  Pallas kernels  97.2 us (86%)
  other arithmetic  8.33 us (7%)
  local copies, waits for them, and re-layouts  3.51 us (3%)
  between operations  2.64 us (2%)
    pallas_call x1, Pallas kernels, refocus(): pl.pallas_call(partial(kernel, count), out_shape=(jax.ShapeDtypeStruct((b...  97.2 us
    unnamed x2, local copies, waits for them, and re-layouts  3.24 us
    concatenate x1, other arithmetic, row_table(): jnp.concatenate([first.astype(jnp.bfloat16), (table - first).astype(jnp.b...  2.53 us

profile of v5, /device:TPU:11, one launch (start us, length us, event | category | flops | bytes accessed | tf_op | source)
XLA Modules:
  0.0 111.7 jit_solution(17608172892139753990)
XLA Ops:
  1.3 0.1 fusion.22
  1.4 0.1 fusion.27
  1.4 2.1 %fusion.29 = (f32[256,1024]{1,0:T(8,128)S(1)}, f32[256,1024]{1,0:T(8,128)S(1)}, f32[256,1024]{1,0:T(8,128)S(1)}) fusion(f32[256,1024]{1,0:T(8,128)} %constant.116.clone, f32[256,1024]{1,0:T(8,128)} %constant.115.clone, f32[1024]{0:T(1024)S(1)} %get-tuple-element.10, f32[256]{0:T(256)S(1)} %get-tuple-element.11, f32[1024]{0:T(1024)S(1)} %get-tuple-element.9, ...), kind=kLoop, calls=%fused_computation.70 | loop fusion | flops 3407872 | bytes 5253120 | tf_op jit(solution)/shard_map/neg | solution.py:55
  3.5 0.5 pad_maximum_fusion.1
  4.0 0.3 maximum_bitcast_fusion
  4.3 0.3 copy.11
  4.5 0.9 reduce-precision_convert_fusion
  5.4 2.5 %pad_maximum_fusion.table_ref = bf16[2,512,2048]{2,1,0:T(8,128)(2,1)} fusion(bf16[2,256,2048]{2,1,0:T(8,128)(2,1)S(1)} %get-tuple-element.3, bf16[2,256,2048]{2,1,0:T(8,128)(2,1)S(1)} %get-tuple-element.2), kind=kLoop, calls=%fused_computation.4 | loop fusion | flops 8388608 | bytes 8388608 | tf_op jit(solution)/shard_map/concatenate | solution.py:62
  8.0 0.7 fusion.9
  8.7 0.7 pad_maximum_fusion.3.phase_ref
  10.6 0.6 maximum_bitcast_fusion.1.smooth_ref
  11.2 97.2 %shard_map.104 = (f32[64,512]{1,0:T(8,128)}, f32[2,64,512]{2,1,0:T(8,128)}) custom-call(f32[1,6]{1,0:T(1,128)} %maximum_bitcast_fusion.1.smooth_ref, bf16[2,512,2048]{2,1,0:T(8,128)(2,1)} %pad_maximum_fusion.table_ref, f32[2,4096]{1,0:T(2,128)} %pad_maximum_fusion.3.phase_ref, f32[2,32,128]{2,1,0:T(8,128)} %constant.117.clone.twist_ref, ...), custom_call_target="tpu_custom_call" | custom-call | tf_op jit(solution)/shard_map/pallas_call | solution.py:478
  108.4 1.6 %copy.17 = f32[64,512]{1,0:T(8,128)} copy(f32[64,512]{1,0:T(8,128)} %get-tuple-element.17) | data formatting | bytes 262144
  110.0 1.7 %copy.18 = f32[2,64,512]{2,1,0:T(8,128)} copy(f32[2,64,512]{2,1,0:T(8,128)} %get-tuple-element.18) | data formatting | bytes 524288
  (1 shorter events, 0.0 us)

commit v6 on v5

--- a/solution.py
+++ b/solution.py
@@ -36,31 +36,23 @@
     return 2 if band // STRIP % 2 == 0 else 1
 
 
-def row_table(plane, place, count):
+def row_order(values, count):
+    band = Y_WIN // count
+    split = values.reshape(count // CORES, CORES, band // STRIP, STRIP, -1)
+    return split.transpose(2, 1, 0, 3, 4).reshape(Y_WIN, -1)
+
+
+def row_phases(plane, place, count):
     freqs_n = NX // count
-    band = Y_WIN // count
     turns = np.arange(Y_WIN)[:, None] * np.arange(freqs_n)[None, :] % NX
-    angle = turns * (2.0 * np.pi / NX)
-    base_cos = jnp.asarray(np.cos(angle).astype(np.float32))
-    base_sin = jnp.asarray(np.sin(angle).astype(np.float32))
+    angle = row_order(turns * (2.0 * np.pi / NX), count)
+    base = np.stack([np.cos(angle), np.sin(angle)]).astype(np.float32)
     phase = line_phase(plane, place * freqs_n + jnp.arange(freqs_n, dtype=jnp.int32))
-    start = place * freqs_n * jnp.arange(Y_WIN, dtype=jnp.int32) % NX
-    start_angle = start.astype(jnp.float32) * (2.0 * math.pi / NX)
-    col_cos, col_sin = jnp.cos(phase)[None, :], jnp.sin(phase)[None, :]
-    row_cos, row_sin = jnp.cos(start_angle)[:, None], jnp.sin(start_angle)[:, None]
-    turn_cos = row_cos * col_cos - row_sin * col_sin
-    turn_sin = row_cos * col_sin + row_sin * col_cos
-    real = base_cos * turn_cos - base_sin * turn_sin
-    imag = base_cos * turn_sin + base_sin * turn_cos
-    upper = jnp.concatenate([real, -imag], axis=1)
-    lower = jnp.concatenate([imag, real], axis=1)
-    table = jnp.stack([upper, lower]).reshape(
-        2, count // CORES, CORES, band // STRIP, STRIP, 2 * freqs_n)
-    table = table.transpose(3, 2, 1, 0, 4, 5)
-    table = table.reshape(band // STRIP // pair_of(band), -1, 2 * freqs_n)
-    first = lax.reduce_precision(table, 8, 7)
-    return jnp.concatenate(
-        [first.astype(jnp.bfloat16), (table - first).astype(jnp.bfloat16)], axis=1)
+    rows = row_order(np.arange(Y_WIN, dtype=np.int32), count)
+    start = (place * freqs_n * jnp.asarray(rows) % NX).astype(jnp.float32)
+    start = start * (2.0 * math.pi / NX)
+    return (jnp.asarray(base), jnp.stack([jnp.cos(phase), jnp.sin(phase)]),
+            jnp.stack([jnp.cos(start), jnp.sin(start)]))
 
 
 def butterflies(real, imag):
@@ -107,8 +99,8 @@
     return jnp.where(lane == edge, 0.0, pltpu.roll(block, shift, block.ndim - 1))
 
 
-def kernel(count, smooth_ref, table_ref, phase_ref, twist_ref, dft_ref, order_ref, spec_ref,
-           map_ref, field_ref, spec, part, core_in, half,
+def kernel(count, smooth_ref, base_ref, turn_ref, start_ref, phase_ref, twist_ref, dft_ref, order_ref, spec_ref,
+           map_ref, field_ref, table, spec, part, core_in, half,
            code_out, unit_out, code_in, unit_in, strip_sum, mid, pic, rim, energy, score,
            send_s, send_q, send_r, recv_s, recv_q, recv_r,
            loads, a_send, a_recv, b_send, b_recv, halo_send, halo_recv, sends, recvs):
@@ -222,14 +214,38 @@
         for i in range(pair):
             pass_on(unit_of(p, c, i))
 
+    def make_table(p):
+        blocks = pair * CORES * chips
+        freqs_n = turn_ref.shape[1]
+        pc, ps = turn_ref[0:1, :], turn_ref[1:2, :]
+
+        @pl.loop(0, blocks)
+        def _(b):
+            rows = pl.ds(pl.multiple_of((p * blocks + b) * STRIP, STRIP), STRIP)
+            bc, bs = base_ref[0, rows, :], base_ref[1, rows, :]
+            rc, rs = start_ref[0, rows, :], start_ref[1, rows, :]
+            tc, ts = rc * pc - rs * ps, rc * ps + rs * pc
+            real, imag = bc * tc - bs * ts, bc * ts + bs * tc
+            at = pl.multiple_of(b * block, block)
+            for value, places in ((real, ((0, 0), (STRIP, freqs_n))),
+                                  (imag, ((STRIP, 0),)), (-imag, ((0, freqs_n),))):
+                first = value.astype(jnp.bfloat16)
+                second = (value - first.astype(jnp.float32)).astype(jnp.bfloat16)
+                for row, lane in places:
+                    lanes = slice(lane, lane + freqs_n)
+                    table[p, pl.ds(at + row, STRIP), lanes] = first
+                    table[p, pl.ds(at + row + blocks * block, STRIP), lanes] = second
+
     def rows_transform(p):
+        make_table(p)
+
         @pl.loop(0, parts_n)
         def _(c):
             @pl.when(p == 0)
             def _():
                 load(c).wait()
 
-            both = jnp.dot(table_ref[p], spec[c], preferred_element_type=jnp.float32)
+            both = jnp.dot(table[p], spec[c], preferred_element_type=jnp.float32)
             for i in range(pair):
                 u = unit_of(p, c, i)
                 low, high = i * part_rows, (pair + i) * part_rows
@@ -241,6 +257,10 @@
                 pass_all(p, c - 1)
 
         pass_all(p, parts_n - 1)
+
+    @pl.loop(0, strips // pair)
+    def _(p):
+        rows_transform(p)
 
     def columns(k):
         rows = pl.ds(pl.multiple_of(chip * block, block), block)
@@ -374,10 +394,6 @@
 
     @pl.loop(0, strips)
     def _(k):
-        @pl.when(k % pair == 0)
-        def _():
-            rows_transform(k // pair)
-
         columns(k)
 
         @pl.when(jnp.logical_and(k == 0, has_low))
@@ -446,7 +462,7 @@
             field_ref[1, rows, :] = placed[2 * STRIP + 8 * n:2 * STRIP + 8 * n + 8]
 
 
-def refocus(smooth, table, phase, spectra, count, targets):
+def refocus(smooth, rows, phase, spectra, count, targets):
     band = Y_WIN // count
     strips = band // STRIP
     groups = SLABS // targets
@@ -455,6 +471,7 @@
     chips = count // CORES
     units = strips * NX // UNIT
     half_rows = chips * 2 * STRIP
+    pair = pair_of(band)
     lane = np.arange(LANES)
     twist = np.arange(SLABS)[:, None] * lane[None, :] * (2.0 * np.pi / NX)
     twist = np.stack([np.cos(twist), np.sin(twist)]).astype(np.float32)
@@ -479,10 +496,12 @@
         partial(kernel, count),
         out_shape=(jax.ShapeDtypeStruct((band, width), jnp.float32),
                    jax.ShapeDtypeStruct((2, band, width), jnp.float32)),
-        in_specs=[pl.BlockSpec(memory_space=pltpu.SMEM)] + [vmem] * 5
+        in_specs=[pl.BlockSpec(memory_space=pltpu.SMEM)] + [vmem] * 7
         + [pl.BlockSpec(memory_space=pl.ANY)],
         out_specs=(vmem, vmem),
         scratch_shapes=[
+            pltpu.VMEM((strips // pair, pair * 2 * CORES * half_rows, spectra.shape[0]),
+                       jnp.bfloat16),
             pltpu.VMEM((NX // UNIT, spectra.shape[0], UNIT), jnp.bfloat16),
             pltpu.VMEM((units, CORES * half_rows, UNIT), jnp.float32),
             pltpu.VMEM((units, half_rows, UNIT), jnp.float32),
@@ -507,7 +526,7 @@
         ],
         compiler_params=pltpu.CompilerParams(
             collective_id=0, has_side_effects=True, vmem_limit_bytes=VMEM_BYTES),
-    )(smooth, table, phase, jnp.asarray(twist), jnp.asarray(dft),
+    )(smooth, *rows, phase, jnp.asarray(twist), jnp.asarray(dft),
       jnp.asarray(order, jnp.bfloat16), spectra)
 
 
@@ -516,7 +535,7 @@
     targets = lax.axis_size("depth")
     place = lax.axis_index("rows")
     plane, radius = plane_index[0], kernel_width[0]
-    table = row_table(plane, place, count)
+    rows = row_phases(plane, place, count)
     spectra = spectrum.reshape(2 * spectrum.shape[1], NX)
     phase = line_phase(plane, jnp.arange(NX, dtype=jnp.int32))
     phase = jnp.stack([jnp.cos(phase), jnp.sin(phase)])
@@ -524,7 +543,7 @@
     smooth = jnp.concatenate([
         (2 * radius + 1).astype(jnp.float32)[None], inside, focus_gain,
         plane_index.astype(jnp.float32) / DEPTHS])[None]
-    return refocus(smooth, table, phase, spectra, count, targets)
+    return refocus(smooth, rows, phase, spectra, count, targets)
 
 
 def solution(mesh):

time: 113 us -> 100 us (0.88); the launches traced: 112 us -> 99.9 us
  Pallas kernels: 97.2 us -> 89.4 us
  other arithmetic: 8.33 us -> 4.32 us
    pallas_call x1, Pallas kernels: 97.2 us -> 89.4 us  [refocus(): pl.pallas_call(partial(kernel, count), out_shape=(jax.ShapeDtypeStruct((b...]
    concatenate x2 -> x0, other arithmetic: 3.02 us -> none  [the longest x1 2.53 us: row_table(): jnp.concatenate([first.astype(jnp.bfloat16), (table - first).astype(jnp.b...]
    neg x1 -> x0, other arithmetic: 2.07 us -> none  [row_table(): upper = jnp.concatenate([real, -imag], axis=1)]
    another operation x0 -> x3, other arithmetic: none -> 2.07 us  [the longest x2 1.46 us: row_phases(): jnp.stack([jnp.cos(start), jnp.sin(start)])]
where the time goes in v6:
time: 100 us; the launch traced here: 99.9 us
  Pallas kernels  89.4 us (89%)
  other arithmetic  4.32 us (4%)
  local copies, waits for them, and re-layouts  3.56 us (4%)
  between operations  2.62 us (3%)
    pallas_call x1, Pallas kernels, refocus(): pl.pallas_call(partial(kernel, count), out_shape=(jax.ShapeDtypeStruct((b...  89.4 us
    unnamed x2, local copies, waits for them, and re-layouts  3.24 us

profile of v6, /device:TPU:11, one launch (start us, length us, event | category | flops | bytes accessed | tf_op | source)
XLA Modules:
  0.0 99.9 jit_solution(14397544351776572399)
XLA Ops:
  2.6 0.7 maximum_bitcast_fusion.smooth_ref
  3.3 0.7 cosine_bitcast_fusion
  4.1 0.2 fusion.18
  4.3 0.6 pad_maximum_fusion.2.turn_ref
  4.9 0.7 fusion.8
  5.6 0.7 pad_maximum_fusion.1.phase_ref
  6.2 0.1 copy.16
  6.4 0.1 copy.15
  6.5 0.7 pad_maximum_fusion.start_ref
  7.2 89.4 %shard_map.104 = (f32[64,512]{1,0:T(8,128)}, f32[2,64,512]{2,1,0:T(8,128)}) custom-call(f32[1,6]{1,0:T(1,128)} %maximum_bitcast_fusion.smooth_ref, f32[2,256,1024]{2,1,0:T(8,128)} %constant.116.clone.base_ref, f32[2,1024]{1,0:T(2,128)} %pad_maximum_fusion.2.turn_ref, f32[2,256,1]{2,1,0:T(8,128)} %pad_maximum_fusion.start_ref, ...), custom_call_target="tpu_custom_call" | custom-call | tf_op jit(solution)/shard_map/pallas_call | solution.py:495
  96.7 1.6 %copy.22 = f32[64,512]{1,0:T(8,128)} copy(f32[64,512]{1,0:T(8,128)} %get-tuple-element.10) | data formatting | bytes 262144
  98.2 1.7 %copy.23 = f32[2,64,512]{2,1,0:T(8,128)} copy(f32[2,64,512]{2,1,0:T(8,128)} %get-tuple-element.11) | data formatting | bytes 524288
  (2 shorter events, 0.1 us)

commit v7 on v6

--- a/solution.py
+++ b/solution.py
@@ -16,7 +16,7 @@
 LANES = 128
 SLABS = NX // LANES
 CORES = 2
-UNIT = 1024
+UNIT = 512
 STRIP = 16
 STEPS = 32767.0
 TINY = 1e-33

time: 100 us -> 101 us (1.010)
  Pallas kernels: 89.4 us -> 90.6 us
    pallas_call x1, Pallas kernels: 89.4 us -> 90.6 us  [refocus(): pl.pallas_call(partial(kernel, count), out_shape=(jax.ShapeDtypeStruct((b...]
where the time goes in v7:
time: 101 us
  Pallas kernels  90.6 us (90%)
  other arithmetic  4.32 us (4%)
  local copies, waits for them, and re-layouts  3.56 us (4%)
  between operations  2.62 us (3%)
    pallas_call x1, Pallas kernels, refocus(): pl.pallas_call(partial(kernel, count), out_shape=(jax.ShapeDtypeStruct((b...  90.6 us
    unnamed x2, local copies, waits for them, and re-layouts  3.24 us

profile of v7, /device:TPU:11, one launch (start us, length us, event | category | flops | bytes accessed | tf_op | source)
XLA Modules:
  0.0 101.1 jit_solution(8835148444480611939)
XLA Ops:
  2.6 0.7 maximum_bitcast_fusion.smooth_ref
  3.3 0.7 cosine_bitcast_fusion
  4.1 0.2 fusion.18
  4.3 0.6 pad_maximum_fusion.2.turn_ref
  4.9 0.7 fusion.8
  5.6 0.7 pad_maximum_fusion.1.phase_ref
  6.2 0.1 copy.16
  6.4 0.1 copy.15
  6.5 0.7 pad_maximum_fusion.start_ref
  7.2 90.6 %shard_map.104 = (f32[64,512]{1,0:T(8,128)}, f32[2,64,512]{2,1,0:T(8,128)}) custom-call(f32[1,6]{1,0:T(1,128)} %maximum_bitcast_fusion.smooth_ref, f32[2,256,1024]{2,1,0:T(8,128)} %constant.116.clone.base_ref, f32[2,1024]{1,0:T(2,128)} %pad_maximum_fusion.2.turn_ref, f32[2,256,1]{2,1,0:T(8,128)} %pad_maximum_fusion.start_ref, ...), custom_call_target="tpu_custom_call" | custom-call | tf_op jit(solution)/shard_map/pallas_call | solution.py:495
  97.9 1.6 %copy.22 = f32[64,512]{1,0:T(8,128)} copy(f32[64,512]{1,0:T(8,128)} %get-tuple-element.10) | data formatting | bytes 262144
  99.5 1.7 %copy.23 = f32[2,64,512]{2,1,0:T(8,128)} copy(f32[2,64,512]{2,1,0:T(8,128)} %get-tuple-element.11) | data formatting | bytes 524288
  (2 shorter events, 0.1 us)
